TPU v7x, 32 devices: a whole 2x2x4 slice. The times are simulated.
32 devices in a mesh: member: 2 (over y), gx: 4 (over z), gy: 2 (over x), gz: 2 (over core).
Axes of the slice: x: 2, y: 2, z: 4, core: 2. Of those that a mesh axis runs over, the one named last changes fastest.
Arguments:
- parent: float32 [6, 40, 16, 512], P('member', None, 'gx', ('gy', 'gz')), parts along dimension 0, may hold values from -6 to 6
- nest: float32 [6, 40, 24, 1536], P('member', None, 'gx', ('gy', 'gz')), parts along dimension 0, may hold values from -6 to 6
- nest_anchor: int32 [2], P('member'), parts along dimension 0, may hold values from 4 to 8
- donor_rows: int32 [8, 2, 4, 1536], P('member', None, None, ('gy', 'gz')), parts along dimension 0, may hold values from 0 to 3
- donor_cols: int32 [8, 2, 4, 1536], P('member', None, None, ('gy', 'gz')), parts along dimension 0, may hold values from -1 to 1
- donor_weights: float32 [8, 2, 4, 1536], P('member', None, None, ('gy', 'gz')), parts along dimension 0, may hold values from 0.05 to 0.45
- wind_x: float32 [40], replicated, may hold values from -0.5 to 0.5
- wind_y: float32 [40], replicated, may hold values from -0.5 to 0.5
- column_mix: float32 [40, 40], replicated, may hold values from -0.25 to 0.25
Outputs:
- parent_out: float32 [6, 40, 16, 512], P('member', None, 'gx', ('gy', 'gz')), parts along dimension 0
- nest_out: float32 [6, 40, 24, 1536], P('member', None, 'gx', ('gy', 'gz')), parts along dimension 0
There are 2 independent parts, one for each index of `member`. A program takes and returns all parts, laid end to end along the dimension named above; an argument that names none is the same for every part. Nothing has to cross between parts.
All inputs are finite; a program needn't handle non-finite values.
Results may differ from a plain program's by a relative error of at most 0.0001.
Values sent between devices are 32-bit elements; how exact they have to be, the bound alone decides.
A program may use at most 128 MiB of HBM per device.

v0:
```python
import jax
import jax.numpy as jnp
from jax import lax
from jax.sharding import PartitionSpec as P

ZR = 4


SOUND = 0.6
DIFFUSE = 0.125


def padded_2(block, sides, width):
    for axis, dim in sides:
        count = lax.axis_size(axis)
        forward = [(i, i + 1) for i in range(count - 1)]
        backward = [(target, source) for source, target in forward]
        low = lax.ppermute(
            lax.slice_in_dim(block, block.shape[dim] - width, None, axis=dim), axis, forward
        )
        high = lax.ppermute(lax.slice_in_dim(block, 0, width, axis=dim), axis, backward)
        block = jnp.concatenate([low, block, high], axis=dim)
    return block


def step_padded(padded, wind_x, wind_y, column_mix):
    centre = padded[:, :, 1:-1, 1:-1]
    east_side = padded[:, :, 2:, 1:-1]
    west_side = padded[:, :, :-2, 1:-1]
    north_side = padded[:, :, 1:-1, 2:]
    south_side = padded[:, :, 1:-1, :-2]
    courant_x = wind_x[None, :, None, None]
    courant_y = wind_y[None, :, None, None]
    advected = (
        centre
        - 0.5 * courant_x * (east_side - west_side)
        - 0.5 * courant_y * (north_side - south_side)
        + DIFFUSE * (east_side + west_side + north_side + south_side - 4.0 * centre)
    )
    speed_u = advected[0] - 0.5 * SOUND * (east_side[2] - west_side[2])
    speed_v = advected[1] - 0.5 * SOUND * (north_side[2] - south_side[2])
    pressure = advected[2] - 0.5 * SOUND * (
        east_side[0] - west_side[0] + (north_side[1] - south_side[1])
    )
    fields = jnp.stack([speed_u, speed_v, pressure])
    return fields + jnp.einsum("lm,kmxy->klxy", column_mix, fields, precision=lax.Precision.HIGHEST)


def sample_zone(zone_rows, donor_rows, donor_cols, donor_weights):
    zone_width = zone_rows.shape[-1]
    half_rows = zone_rows.shape[-2] // 2
    nest_cols = donor_rows.shape[-1]
    col_index = jnp.arange(nest_cols, dtype=jnp.int32)[None, None, None, :] // 3 + donor_cols + 1
    edge_index = jnp.arange(2, dtype=jnp.int32)[None, :, None, None]
    flat_index = (edge_index * half_rows + donor_rows) * zone_width + col_index
    flattened = zone_rows.reshape(zone_rows.shape[:-2] + (zone_rows.shape[-2] * zone_width,))
    picked = jnp.take(flattened, flat_index, axis=-1)
    return jnp.sum(picked * donor_weights, axis=-4)


def fix_edges(extended, bounds, substep, row_start, col_start, total_rows, total_cols):
    fraction = substep / 3.0
    blended = (1.0 - fraction) * bounds[0] + fraction * bounds[1]
    edge_rows = blended.shape[3]
    global_rows = row_start + jnp.arange(extended.shape[2], dtype=jnp.int32)
    global_cols = col_start + jnp.arange(extended.shape[3], dtype=jnp.int32)
    west_values = jnp.take(blended[:, :, 0], jnp.clip(global_rows, 0, edge_rows - 1), axis=2)
    east_values = jnp.take(
        blended[:, :, 1], jnp.clip(global_rows - (total_rows - edge_rows), 0, edge_rows - 1), axis=2
    )
    row_shape = global_rows[None, None, :, None]
    col_shape = global_cols[None, None, None, :]
    result = jnp.where(
        row_shape < edge_rows,
        west_values,
        jnp.where(row_shape >= total_rows - edge_rows, east_values, extended),
    )
    inside = (
        (row_shape >= 0) & (row_shape < total_rows) & (col_shape >= 0) & (col_shape < total_cols)
    )
    return jnp.where(inside, result, 0.0)


def shards(
    parent, nest, nest_anchor, donor_rows, donor_cols, donor_weights, wind_x, wind_y, column_mix
):
    anchor = nest_anchor[0]
    levels = parent.shape[1]
    parent_rows = parent.shape[2]
    nest_rows = nest.shape[2]
    nest_cols = nest.shape[3]
    tiles_x = lax.axis_size("gx")
    block_x = lax.axis_index("gx")
    block_y = lax.axis_index(("gy", "gz"))
    total_parent = parent_rows * tiles_x
    total_nest = nest_rows * tiles_x
    total_nest_cols = nest_cols * lax.axis_size(("gy", "gz"))
    padded = padded_2(parent, (("gx", 2), (("gy", "gz"), 3)), 1)
    parent_new = step_padded(padded, wind_x, wind_y, column_mix)
    starts = (anchor, anchor + total_parent // 2 - ZR)
    span_rows = ZR + 2
    wanted = jnp.concatenate(
        [
            starts[0] - 1 + jnp.arange(span_rows, dtype=jnp.int32),
            starts[1] - 1 + jnp.arange(span_rows, dtype=jnp.int32),
        ]
    )
    rimmed = padded[:, :, 1:-1, :]
    piece = lax.all_gather(rimmed, "gx", axis=2, tiled=True)
    piece_rows = piece.shape[2]
    select = (wanted[:, None] == jnp.arange(piece_rows, dtype=jnp.int32)[None, :]).astype(
        jnp.float32
    )
    extended_rows = jnp.einsum("zc,klcy->klzy", select, piece, precision=lax.Precision.HIGHEST)
    west_block = extended_rows[:, :, :span_rows]
    east_block = extended_rows[:, :, span_rows:]
    old_zone = jnp.concatenate([west_block[:, :, 1:-1, 1:-1], east_block[:, :, 1:-1, 1:-1]], axis=2)
    new_zone = jnp.concatenate(
        [
            step_padded(west_block, wind_x, wind_y, column_mix),
            step_padded(east_block, wind_x, wind_y, column_mix),
        ],
        axis=2,
    )
    zone_rows = jnp.stack([old_zone, new_zone])
    zone_wide = padded_2(zone_rows, ((("gy", "gz"), 4),), 1)
    bounds = sample_zone(zone_wide, donor_rows, donor_cols, donor_weights)
    nest_state = nest
    for substep in range(1, 4):
        nest_padded = padded_2(nest_state, (("gx", 2), (("gy", "gz"), 3)), 1)
        nest_state = step_padded(nest_padded, wind_x, wind_y, column_mix)
        nest_state = fix_edges(
            nest_state,
            bounds,
            substep,
            block_x * nest_rows,
            block_y * nest_cols,
            total_nest,
            total_nest_cols,
        )
    coarse = nest_state.reshape(3, levels, nest_rows // 3, 3, nest_cols // 3, 3).mean(axis=(3, 5))
    parent_global = block_x * parent_rows + jnp.arange(parent_rows, dtype=jnp.int32)
    footprint = total_parent // 2
    piece = lax.all_gather(coarse, "gx", axis=2, tiled=True)
    piece_rows = piece.shape[2]
    coarse_index = jnp.arange(piece_rows, dtype=jnp.int32)
    usable = (coarse_index >= 1) & (coarse_index <= footprint - 2)
    select = ((parent_global[:, None] == anchor + coarse_index[None, :]) & usable[None, :]).astype(
        jnp.float32
    )
    placed = jnp.einsum("rc,klcy->klry", select, piece, precision=lax.Precision.HIGHEST)
    covered = jnp.sum(select, axis=1)
    parent_out = jnp.where(covered[None, None, :, None] > 0.5, placed, parent_new)
    return (parent_out, nest_state)


def solution(mesh):
    placed = (
        P("member", None, "gx", ("gy", "gz")),
        P("member", None, "gx", ("gy", "gz")),
        P("member"),
        P("member", None, None, ("gy", "gz")),
        P("member", None, None, ("gy", "gz")),
        P("member", None, None, ("gy", "gz")),
        P(),
        P(),
        P(),
    )
    return jax.shard_map(
        shards,
        mesh=mesh,
        in_specs=placed,
        out_specs=(P("member", None, "gx", ("gy", "gz")), P("member", None, "gx", ("gy", "gz"))),
        check_vma=False,
    )
```

profile of v0, /device:TPU:18, one launch (start us, length us, event | category | flops | bytes accessed | tf_op | source)
XLA Modules:
  0.0 406.2 jit_solution(3469522089369881358)
XLA Ops:
  1.9 3.5 collective-permute-start
  5.4 2.4 collective-permute-start.1
  9.5 3.5 collective-permute-start.7
  13.0 2.4 collective-permute-start.6
  22.2 3.6 collective-permute-start.3
  25.9 4.5 %collective-permute-done.2 = f32[3,40,6,1]{3,2,1,0:T(8,128)S(1)} collective-permute-done((f32[3,40,6,1]{3,2,1,0:T(8,128)S(1)}, f32[3,40,6,1]{3,2,1,0:T(8,128)S(1)}, u32[]{:S(2)}, u32[]{:S(2)}) %collective-permute-start.2) | collective-permute-done | bytes 2912 | tf_op jit(solution)/shard_map/ppermute | solution.py:18
  33.2 30.5 %all_gather.6 = f32[3,40,16,130]{3,1,0,2:T(8,128)S(1)} all-gather(f32[3,40,4,130]{3,1,0,2:T(8,128)S(1)} %copy.54), channel_id=1, replica_groups=mesh['member'=2,'gx'=4,'gy'=2,'gz'=2] {'gx'}, dimensions={2}, use_global_device_ids=true | all-gather | bytes 1248000 | tf_op jit(solution)/shard_map/all_gather | solution.py:109
  73.7 3.8 collective-permute-start.5
  80.5 2.1 pad_maximum_fusion
  82.6 5.7 %copy.81 = f32[2,3,40,8,130]{2,0,4,3,1:T(2,128)S(1)} copy(f32[2,3,40,8,130]{4,3,2,1,0:T(8,128)} %pad_maximum_fusion) | data formatting | bytes 1996800 | tf_op jit(solution)/shard_map/reshape | solution.py:56
  88.4 128.1 %gather_fusion = f32[12288,2,3,40]{3,1,2,0:T(2,128)} fusion(f32[2,3,40,1040]{2,0,3,1:T(2,128)S(1)} %bitcast.114, s32[12288]{0:T(1024)} %broadcast_clamp_fusion), kind=kCustom, calls=%fused_computation.6 | custom fusion | bytes 23642112 | tf_op jit(solution)/shard_map/jit(_take)/gather | solution.py:57
  216.4 63.1 %multiply_reduce_fusion = f32[2,4,384,2,3,40]{5,3,4,2,1,0:T(2,128)} fusion(f32[4,2,4,384,2,3,40]{6,4,5,3,2,1,0:T(2,128)} %bitcast.115, pred[4,2,4,384]{3,2,1,0:T(4,128)(4,1)S(1)} %get-tuple-element.3, f32[4,2,4,384]{3,2,1,0:T(4,128)} %param.16), kind=kLoop, calls=%fused_computation.7 | loop fusion | flops 8110080 | bytes 14807040 | tf_op jit(solution)/shard_map/reduce_sum | solution.py:58
  279.6 11.5 %copy.65 = f32[2,4,384,2,3,40]{2,5,1,4,0,3:T(8,128)S(1)} copy(f32[2,4,384,2,3,40]{5,3,4,2,1,0:T(2,128)} %multiply_reduce_fusion) | data formatting | bytes 5898240 | tf_op jit(solution)/shard_map/reduce_sum | solution.py:58
  296.6 2.4 collective-permute-start.8
  299.0 2.9 collective-permute-start.9
  303.1 2.7 gather_fusion.5
  305.9 2.7 gather_fusion.6
  309.5 2.7 multiply_add_fusion.2
  315.7 3.0 collective-permute-start.10
  318.6 3.0 collective-permute-start.11
  323.7 2.3 collective-permute-done.11
  327.2 2.7 collective-permute-start.12
  336.6 3.8 collective-permute-done.13
  347.1 3.2 collective-permute-start.14
  350.3 2.6 collective-permute-start.15
  354.5 3.2 collective-permute-done.15
  360.8 2.7 collective-permute-start.17
  367.4 3.8 collective-permute-done.17
  377.9 2.5 copy.72
  380.4 6.4 %reshape.166 = f32[3,40,2,3,128,3]{1,5,4,3,2,0:T(4,128)} reshape(f32[3,40,6,384]{1,3,2,0:T(8,128)} %copy.72) | data formatting | bytes 2211840 | tf_op jit(solution)/shard_map/reshape | solution.py:141
  386.8 4.0 reduce_sum.29
  391.1 13.9 %all_gather.7 = f32[3,40,8,128]{3,1,0,2:T(8,128)S(1)} all-gather(f32[3,40,2,128]{3,1,0,2:T(8,128)S(1)} %copy.74), channel_id=1, replica_groups=mesh['member'=2,'gx'=4,'gy'=2,'gz'=2] {'gx'}, dimensions={2}, use_global_device_ids=true | all-gather | bytes 614400 | tf_op jit(solution)/shard_map/all_gather | solution.py:144
  (184 shorter events, 68.3 us)
Async XLA Ops:
  0.6 66.3 %copy-start = (f32[40,40]{1,0:T(8,128)S(1)}, f32[40,40]{1,0:T(8,128)}, u32[]{:S(2)}) copy-start(f32[40,40]{1,0:T(8,128)} %param.19) | copy-start | bytes 19204
  0.6 19.2 %copy-start.5 = (f32[3,40,4,128]{3,2,1,0:T(4,128)S(1)}, f32[3,40,4,128]{3,2,1,0:T(4,128)}, u32[]{:S(2)}) copy-start(f32[3,40,4,128]{3,2,1,0:T(4,128)} %param.11) | copy-start | bytes 737284
  0.7 19.1 %copy-start.37 = (f32[40]{0:T(128)S(1)}, f32[40]{0:T(128)}, u32[]{:S(2)}) copy-start(f32[40]{0:T(128)} %param.17) | copy-start | bytes 484
  0.7 19.1 %copy-start.36 = (f32[40]{0:T(128)S(1)}, f32[40]{0:T(128)}, u32[]{:S(2)}) copy-start(f32[40]{0:T(128)} %param.18) | copy-start | bytes 484
  1.9 18.0 %collective-permute-start = (f32[3,40,1,128]{3,2,1,0:T(1,128)S(1)}, f32[3,40,1,128]{3,2,1,0:T(1,128)S(1)}, u32[]{:S(2)}, u32[]{:S(2)}) collective-permute-start(f32[3,40,1,128]{3,2,1,0:T(1,128)S(1)} %get-tuple-element.56), channel_id=1, source_target_pairs={{0,4},{4,8},{8,12},{1,5},{5,9},{9,13},{2,6},{6,10},{10,14},{3,7},{... | collective-permute-start | bytes 184328 | tf_op jit(solution)/shard_map/ppermute | solution.py:18
  5.4 14.5 %collective-permute-start.1 = (f32[3,40,1,128]{3,2,1,0:T(1,128)S(1)}, f32[3,40,1,128]{3,2,1,0:T(1,128)S(1)}, u32[]{:S(2)}, u32[]{:S(2)}) collective-permute-start(f32[3,40,1,128]{3,2,1,0:T(1,128)S(1)} %get-tuple-element.57), channel_id=1, source_target_pairs={{4,0},{8,4},{12,8},{5,1},{9,5},{13,9},{6,2},{10,6},{14,10},{7,3},{... | collective-permute-start | bytes 184328 | tf_op jit(solution)/shard_map/ppermute | solution.py:21
  9.5 283.5 %collective-permute-start.7 = (f32[3,40,1,384]{3,1,2,0:T(8,128)}, f32[3,40,1,384]{3,1,2,0:T(8,128)}, u32[]{:S(2)}, u32[]{:S(2)}) collective-permute-start(f32[3,40,1,384]{3,1,2,0:T(8,128)} %get-tuple-element.49), channel_id=1, source_target_pairs={{0,4},{4,8},{8,12},{1,5},{5,9},{9,13},{2,6},{6,10},{10,14},{3,7},{... | collective-permute-start | bytes 552968 | tf_op jit(solution)/shard_map/ppermute | solution.py:18
  13.0 281.2 %collective-permute-start.6 = (f32[3,40,1,384]{3,1,2,0:T(8,128)}, f32[3,40,1,384]{3,1,2,0:T(8,128)}, u32[]{:S(2)}, u32[]{:S(2)}) collective-permute-start(f32[3,40,1,384]{3,1,2,0:T(8,128)} %get-tuple-element.48), channel_id=1, source_target_pairs={{4,0},{8,4},{12,8},{5,1},{9,5},{13,9},{6,2},{10,6},{14,10},{7,3},{... | collective-permute-start | bytes 552968 | tf_op jit(solution)/shard_map/ppermute | solution.py:21
  19.9 58.7 %copy-start.17 = (f32[3,40,1,128]{3,2,1,0:T(1,128)}, f32[3,40,1,128]{3,2,1,0:T(1,128)S(1)}, u32[]{:S(2)}) copy-start(f32[3,40,1,128]{3,2,1,0:T(1,128)S(1)} %collective-permute-done.1) | copy-start | bytes 184324
  20.3 10.1 %collective-permute-start.2 = (f32[3,40,6,1]{3,2,1,0:T(8,128)S(1)}, f32[3,40,6,1]{3,2,1,0:T(8,128)S(1)}, u32[]{:S(2)}, u32[]{:S(2)}) collective-permute-start(f32[3,40,6,1]{3,2,1,0:T(8,128)S(1)} %get-tuple-element.54), channel_id=1, source_target_pairs={{0,1},{1,2},{2,3},{4,5},{5,6},{6,7},{8,9},{9,10},{10,11},{12,13},{... | collective-permute-start | bytes 8648 | tf_op jit(solution)/shard_map/ppermute | solution.py:18
  22.2 10.0 %collective-permute-start.3 = (f32[3,40,6,1]{3,2,1,0:T(8,128)S(1)}, f32[3,40,6,1]{3,2,1,0:T(8,128)S(1)}, u32[]{:S(2)}, u32[]{:S(2)}) collective-permute-start(f32[3,40,6,1]{3,2,1,0:T(8,128)S(1)} %get-tuple-element.55), channel_id=1, source_target_pairs={{1,0},{2,1},{3,2},{5,4},{6,5},{7,6},{9,8},{10,9},{11,10},{13,12},{... | collective-permute-start | bytes 8648 | tf_op jit(solution)/shard_map/ppermute | solution.py:21
  30.4 48.1 %copy-start.1 = (f32[3,40,6,1]{3,2,1,0:T(8,128)}, f32[3,40,6,1]{3,2,1,0:T(8,128)S(1)}, u32[]{:S(2)}) copy-start(f32[3,40,6,1]{3,2,1,0:T(8,128)S(1)} %collective-permute-done.2) | copy-start | bytes 8644
  32.2 46.4 %copy-start.3 = (f32[3,40,6,1]{3,2,1,0:T(8,128)}, f32[3,40,6,1]{3,2,1,0:T(8,128)S(1)}, u32[]{:S(2)}) copy-start(f32[3,40,6,1]{3,2,1,0:T(8,128)S(1)} %collective-permute-done.3) | copy-start | bytes 8644
  71.3 8.3 %collective-permute-start.4 = (f32[2,3,40,8,1]{2,3,4,1,0:T(8,128)S(1)}, f32[2,3,40,8,1]{2,3,4,1,0:T(8,128)S(1)}, u32[]{:S(2)}, u32[]{:S(2)}) collective-permute-start(f32[2,3,40,8,1]{2,3,4,1,0:T(8,128)S(1)} %copy.60), channel_id=1, source_target_pairs={{0,1},{1,2},{2,3},{4,5},{5,6},{6,7},{8,9},{9,10},{10,11},{12,13},{... | collective-permute-start | bytes 23048 | tf_op jit(solution)/shard_map/ppermute | solution.py:18
  73.7 6.4 %collective-permute-start.5 = (f32[2,3,40,8,1]{2,3,4,1,0:T(8,128)S(1)}, f32[2,3,40,8,1]{2,3,4,1,0:T(8,128)S(1)}, u32[]{:S(2)}, u32[]{:S(2)}) collective-permute-start(f32[2,3,40,8,1]{2,3,4,1,0:T(8,128)S(1)} %copy.61), channel_id=1, source_target_pairs={{1,0},{2,1},{3,2},{5,4},{6,5},{7,6},{9,8},{10,9},{11,10},{13,12},{... | collective-permute-start | bytes 23048 | tf_op jit(solution)/shard_map/ppermute | solution.py:21
  296.6 12.0 %collective-permute-start.8 = (f32[3,40,8,1]{3,1,2,0:T(8,128)}, f32[3,40,8,1]{3,1,2,0:T(8,128)}, u32[]{:S(2)}, u32[]{:S(2)}) collective-permute-start(f32[3,40,8,1]{3,1,2,0:T(8,128)} %get-tuple-element.39), channel_id=1, source_target_pairs={{1,0},{2,1},{3,2},{5,4},{6,5},{7,6},{9,8},{10,9},{11,10},{13,12},{... | collective-permute-start | bytes 11528 | tf_op jit(solution)/shard_map/ppermute | solution.py:21
  299.0 10.5 %collective-permute-start.9 = (f32[3,40,8,1]{3,1,2,0:T(8,128)}, f32[3,40,8,1]{3,1,2,0:T(8,128)}, u32[]{:S(2)}, u32[]{:S(2)}) collective-permute-start(f32[3,40,8,1]{3,1,2,0:T(8,128)} %get-tuple-element.40), channel_id=1, source_target_pairs={{0,1},{1,2},{2,3},{4,5},{5,6},{6,7},{8,9},{9,10},{10,11},{12,13},{... | collective-permute-start | bytes 11528 | tf_op jit(solution)/shard_map/ppermute | solution.py:18
  315.7 8.1 %collective-permute-start.10 = (f32[3,40,1,384]{3,1,2,0:T(8,128)S(1)}, f32[3,40,1,384]{3,1,2,0:T(8,128)S(1)}, u32[]{:S(2)}, u32[]{:S(2)}) collective-permute-start(f32[3,40,1,384]{3,1,2,0:T(8,128)S(1)} %get-tuple-element.44), channel_id=1, source_target_pairs={{4,0},{8,4},{12,8},{5,1},{9,5},{13,9},{6,2},{10,6},{14,10},{7,3},{... | collective-permute-start | bytes 552968 | tf_op jit(solution)/shard_map/ppermute | solution.py:21
  318.6 7.4 %collective-permute-start.11 = (f32[3,40,1,384]{3,1,2,0:T(8,128)S(1)}, f32[3,40,1,384]{3,1,2,0:T(8,128)S(1)}, u32[]{:S(2)}, u32[]{:S(2)}) collective-permute-start(f32[3,40,1,384]{3,1,2,0:T(8,128)S(1)} %get-tuple-element.43), channel_id=1, source_target_pairs={{0,4},{4,8},{8,12},{1,5},{5,9},{9,13},{2,6},{6,10},{10,14},{3,7},{... | collective-permute-start | bytes 552968 | tf_op jit(solution)/shard_map/ppermute | solution.py:18
  327.2 9.4 %collective-permute-start.12 = (f32[3,40,8,1]{3,1,2,0:T(8,128)}, f32[3,40,8,1]{3,1,2,0:T(8,128)S(1)}, u32[]{:S(2)}, u32[]{:S(2)}) collective-permute-start(f32[3,40,8,1]{3,1,2,0:T(8,128)} %get-tuple-element.35), channel_id=1, source_target_pairs={{1,0},{2,1},{3,2},{5,4},{6,5},{7,6},{9,8},{10,9},{11,10},{13,12},{... | collective-permute-start | bytes 11528 | tf_op jit(solution)/shard_map/ppermute | solution.py:21
  329.9 10.5 %collective-permute-start.13 = (f32[3,40,8,1]{3,1,2,0:T(8,128)}, f32[3,40,8,1]{3,1,2,0:T(8,128)}, u32[]{:S(2)}, u32[]{:S(2)}) collective-permute-start(f32[3,40,8,1]{3,1,2,0:T(8,128)} %get-tuple-element.36), channel_id=1, source_target_pairs={{0,1},{1,2},{2,3},{4,5},{5,6},{6,7},{8,9},{9,10},{10,11},{12,13},{... | collective-permute-start | bytes 11528 | tf_op jit(solution)/shard_map/ppermute | solution.py:18
  347.1 7.4 %collective-permute-start.14 = (f32[3,40,1,384]{3,1,2,0:T(8,128)S(1)}, f32[3,40,1,384]{3,1,2,0:T(8,128)S(1)}, u32[]{:S(2)}, u32[]{:S(2)}) collective-permute-start(f32[3,40,1,384]{3,1,2,0:T(8,128)S(1)} %get-tuple-element.42), channel_id=1, source_target_pairs={{4,0},{8,4},{12,8},{5,1},{9,5},{13,9},{6,2},{10,6},{14,10},{7,3},{... | collective-permute-start | bytes 552968 | tf_op jit(solution)/shard_map/ppermute | solution.py:21
  350.3 7.4 %collective-permute-start.15 = (f32[3,40,1,384]{3,1,2,0:T(8,128)S(1)}, f32[3,40,1,384]{3,1,2,0:T(8,128)S(1)}, u32[]{:S(2)}, u32[]{:S(2)}) collective-permute-start(f32[3,40,1,384]{3,1,2,0:T(8,128)S(1)} %get-tuple-element.41), channel_id=1, source_target_pairs={{0,4},{4,8},{8,12},{1,5},{5,9},{9,13},{2,6},{6,10},{10,14},{3,7},{... | collective-permute-start | bytes 552968 | tf_op jit(solution)/shard_map/ppermute | solution.py:18
  358.8 8.6 %collective-permute-start.16 = (f32[3,40,8,1]{3,1,2,0:T(8,128)}, f32[3,40,8,1]{3,1,2,0:T(8,128)S(1)}, u32[]{:S(2)}, u32[]{:S(2)}) collective-permute-start(f32[3,40,8,1]{3,1,2,0:T(8,128)} %get-tuple-element.29), channel_id=1, source_target_pairs={{1,0},{2,1},{3,2},{5,4},{6,5},{7,6},{9,8},{10,9},{11,10},{13,12},{... | collective-permute-start | bytes 11528 | tf_op jit(solution)/shard_map/ppermute | solution.py:21
  360.8 10.5 %collective-permute-start.17 = (f32[3,40,8,1]{3,1,2,0:T(8,128)}, f32[3,40,8,1]{3,1,2,0:T(8,128)}, u32[]{:S(2)}, u32[]{:S(2)}) collective-permute-start(f32[3,40,8,1]{3,1,2,0:T(8,128)} %get-tuple-element.30), channel_id=1, source_target_pairs={{0,1},{1,2},{2,3},{4,5},{5,6},{6,7},{8,9},{9,10},{10,11},{12,13},{... | collective-permute-start | bytes 11528 | tf_op jit(solution)/shard_map/ppermute | solution.py:18
  390.8 14.2 %copy-start.21 = (f32[3,4,128,40]{2,3,1,0:T(8,128)S(1)}, f32[3,4,128,40]{2,3,1,0:T(8,128)}, u32[]{:S(2)}) copy-start(f32[3,4,128,40]{2,3,1,0:T(8,128)} %fusion.75) | copy-start | bytes 737284
  390.8 14.1 %copy-start.24 = (f32[1,40,4,128]{3,2,1,0:T(4,128)S(1)}, f32[1,40,4,128]{3,2,1,0:T(4,128)}, u32[]{:S(2)}) copy-start(f32[1,40,4,128]{3,2,1,0:T(4,128)} %get-tuple-element.52) | copy-start | bytes 245764
  390.9 14.1 %copy-start.26 = (f32[1,40,4,128]{3,2,1,0:T(4,128)S(1)}, f32[1,40,4,128]{3,2,1,0:T(4,128)}, u32[]{:S(2)}) copy-start(f32[1,40,4,128]{3,2,1,0:T(4,128)} %get-tuple-element.53) | copy-start | bytes 245764
  390.9 14.1 %copy-start.28 = (f32[1,40,4,128]{3,2,1,0:T(4,128)S(1)}, f32[1,40,4,128]{3,2,1,0:T(4,128)}, u32[]{:S(2)}) copy-start(f32[1,40,4,128]{3,2,1,0:T(4,128)} %copy-done.27) | copy-start | bytes 245764
  390.9 14.1 %copy-start.30 = (pred[8]{0:T(512)(128)(4,1)S(1)}, pred[8]{0:T(512)(128)(4,1)}, u32[]{:S(2)}) copy-start(pred[8]{0:T(512)(128)(4,1)} %copy-done.29) | copy-start | bytes 28
  390.9 14.1 %copy-start.32 = (s32[4]{0:T(128)S(1)}, s32[4]{0:T(128)}, u32[]{:S(2)}) copy-start(s32[4]{0:T(128)} %copy-done.31) | copy-start | bytes 52
  390.9 14.1 %copy-start.34 = (s32[8]{0:T(128)S(1)}, s32[8]{0:T(128)}, u32[]{:S(2)}) copy-start(s32[8]{0:T(128)} %copy-done.33) | copy-start | bytes 100
  (29 other events, 116.9 us)
where the time goes:
time: 411 us; the launch traced here: 406 us
  local copies, waits for them, and re-layouts  178 us (43%)
  other arithmetic  101 us (25%)
  starting transfers between devices  49.3 us (12%)
  blocking collectives  44.4 us (11%)
  waiting for transfers between devices  22.8 us (6%)
  matrix products  8.64 us (2%)
    gather x1, local copies, waits for them, and re-layouts, sample_zone(): picked = jnp.take(flattened, flat_index, axis=-1)  128 us
    reduce_sum x1, other arithmetic, sample_zone(): return jnp.sum(picked * donor_weights, axis=-4)  63.1 us
    all_gather x1, blocking collectives, shards(): piece = lax.all_gather(rimmed, 'gx', axis=2, tiled=True)  30.5 us
    ppermute x9, starting transfers between devices, padded_2(): lax.ppermute(lax.slice_in_dim(block, 0, width, axis=dim), axis, backward)  25.4 us
    ppermute x9, starting transfers between devices, padded_2(): lax.ppermute(lax.slice_in_dim(block, block.shape[dim] - width, None, axis...  23.9 us
    ppermute x9, waiting for transfers between devices, padded_2(): lax.ppermute(lax.slice_in_dim(block, block.shape[dim] - width, None, axis...  18.6 us
    all_gather x1, blocking collectives, shards(): piece = lax.all_gather(coarse, 'gx', axis=2, tiled=True)  13.9 us
    reduce_sum x1, local copies, waits for them, and re-layouts, sample_zone(): return jnp.sum(picked * donor_weights, axis=-4)  11.5 us
  transfers between devices with their start and end apart: 18, of which 10 were waited for; matrix products, arithmetic and copies ran while one was open for 61% of the time, Pallas kernels for 0%

commit v1 on v0

v1 whole, which is shorter than its diff:
```python
import functools

import jax
import jax.numpy as jnp
from jax import lax
from jax.experimental import pallas as pl
from jax.experimental.pallas import tpu as pltpu
from jax.sharding import PartitionSpec as P

MESH = pl.DeviceIdType.MESH
F32 = jnp.float32
BF16 = jnp.bfloat16
T = 128
H = 3
WEST, EAST = 0, 1


def lanes(shape, dim=1):
    return lax.broadcasted_iota(jnp.int32, shape, dim)


def split(x):
    hi = x.astype(BF16)
    lo = (x - hi.astype(F32)).astype(BF16)
    return hi, lo


def kernel(
    X, Y, CY,
    parent, nest, anchor, d_rows, d_cols, d_wts, coef, mixer,
    parent_out, nest_out,
    edge, pb, phb, hl, hh, px, sa, sb, send_w, recv_w, zb, zn, grid, wx, wrb, wxb, b0, b1, co, cb,
    pack_ss, pack_rs, ph_ss, ph_rs, halo_ss, halo_rs, win_ss, win_rs, wt_ss, wt_rs, co_ss, co_rs,
):
    R = parent.shape[1]
    N = nest.shape[1]
    LEV = nest.shape[2]
    C = nest.shape[3]
    W = C + T
    me = lax.axis_index("member")
    ix = lax.axis_index("gx")
    iy = lax.axis_index("gy") * CY + lax.axis_index("gz")
    half = X // 2
    is_west = ix == 0
    is_east = ix == X - 1
    has_col = (iy > 0, iy < Y - 1)

    def dev(x, y):
        return (me, x, y // CY, lax.rem(y, CY))

    def rcopy(src, dst, ss, rs, x, y):
        return pltpu.make_async_remote_copy(
            src_ref=src, dst_ref=dst, send_sem=ss, recv_sem=rs, device_id=dev(x, y), device_id_type=MESH
        )

    def arrived(ref, rs):
        rcopy(ref, ref, halo_ss.at[0], rs, lax.rem(ix + 1, X), iy).wait_recv()

    def col_partner(side):
        return iy + (1 if side else -1)

    def row_ok(dx):
        return (ix + dx >= 0) & (ix + dx < X)

    barrier = pltpu.get_barrier_semaphore()
    for m in range(1, X):
        pl.semaphore_signal(barrier, inc=1, device_id=dev(lax.rem(ix + m, X), iy), device_id_type=MESH)
    near = jnp.int32(X - 1)
    for side in (0, 1):
        for dx in (-1, 0, 1):
            there = has_col[side] & row_ok(dx)
            near = near + there.astype(jnp.int32)

            @pl.when(there)
            def _():
                pl.semaphore_signal(
                    barrier, inc=1, device_id=dev(ix + dx, col_partner(side)), device_id_type=MESH
                )

    lane = lanes((LEV, T))
    edge[...] = jnp.zeros_like(edge)

    def pack_nest(n, carry):
        spot = (lane >= H * n) & (lane < H * n + H)
        k, r = n // N, lax.rem(n, N)
        left = nest[k, r, :, 0:T]
        right = nest[k, r, :, C - T : C]
        edge[0] = jnp.where(spot, pltpu.roll(left, H * n, 1), edge[0])
        edge[1] = jnp.where(spot, pltpu.roll(right, lax.rem(H * n + H, T), 1), edge[1])
        return carry

    def pack_parent(n, carry):
        spot = (lane >= 64 + H * n) & (lane < 64 + H * n + H)
        v = parent[n // R, lax.rem(n, R)]
        edge[0] = jnp.where(spot, pltpu.roll(v, 64 + H * n, 1), edge[0])
        edge[1] = jnp.where(spot, pltpu.roll(v, 64 + H * n + H, 1), edge[1])
        return carry

    lax.fori_loop(0, 3 * N, pack_nest, 0)
    lax.fori_loop(0, 3 * R, pack_parent, 0)

    pl.semaphore_wait(barrier, near)

    def pack_copy(side, dx):
        return rcopy(
            edge.at[side], pb.at[1 - dx, 1 - side], pack_ss.at[dx + 1, side], pack_rs.at[1 - dx, 1 - side],
            ix + dx, col_partner(side),
        )

    def ph_copy(down):
        if down:
            return rcopy(parent.at[:, 0], phb.at[1], ph_ss.at[1], ph_rs.at[1], ix - 1, iy)
        return rcopy(parent.at[:, R - 1], phb.at[0], ph_ss.at[0], ph_rs.at[0], ix + 1, iy)

    def halo_copy(down):
        if down:
            return rcopy(nest.at[:, 0:H], hh, halo_ss.at[1], halo_rs.at[1], ix - 1, iy)
        return rcopy(nest.at[:, N - H : N], hl, halo_ss.at[0], halo_rs.at[0], ix + 1, iy)

    for dx in (0, -1, 1):
        for side in (0, 1):
            there = has_col[side] & row_ok(dx)
            pl.when(there)(lambda: pack_copy(side, dx).start())
            pl.when(jnp.logical_not(there))(
                lambda: pb.__setitem__((dx + 1, side), jnp.zeros((LEV, T), F32))
            )
    pl.when(ix > 0)(lambda: ph_copy(True).start())
    pl.when(ix < X - 1)(lambda: ph_copy(False).start())
    early_down = (ix == 1) | (ix > half + 1)
    pl.when(early_down)(lambda: halo_copy(True).start())
    pl.when(ix < X - 1)(lambda: halo_copy(False).start())

    def pack_wait(dx):
        for side in (0, 1):
            pl.when(has_col[side] & row_ok(dx))(
                lambda: arrived(pb.at[dx + 1, side], pack_rs.at[dx + 1, side])
            )

    pack_wait(0)

    rim_spot = (lane < H) | (lane >= T - H)

    def unpack(dx, off):
        left = pltpu.roll(pb[dx + 1, 0], lax.rem(2 * T - H - off, T), 1)
        right = pltpu.roll(pb[dx + 1, 1], lax.rem(T - off, T), 1)
        return jnp.where(rim_spot, jnp.where(lane < T // 2, right, left), 0.0)

    def take_parent(n, carry):
        k, r = n // R, lax.rem(n, R)
        px[k, r + 1, :, 0:T] = parent[k, r]
        px[k, r + 1, :, T : 2 * T] = unpack(0, 64 + H * n)
        return carry

    lax.fori_loop(0, 3 * R, take_parent, 0)

    a0 = jnp.full((LEV, T), anchor[0], jnp.int32)
    first = (a0 - 1, a0 + (R * X // 2 - 4 - 1))

    def share(which):
        base = 1 if which else 0
        rims = 0 if which else 18

        def one(n, acc):
            t, k = n // 3, lax.rem(n, 3)
            body = jnp.zeros((LEV, T), F32)
            rim = jnp.zeros((LEV, T), F32)
            for i in range(R):
                hit = first[which] + t == R * ix + i
                body = jnp.where(hit, px[k, i + 1, :, 0:T], body)
                rim = jnp.where(hit, px[k, i + 1, :, T : 2 * T], rim)
            send_w[which, base + n] = body
            spot = (lane >= 6 * n) & (lane < 6 * n + 6)
            return jnp.where(spot, pltpu.roll(rim, lax.rem(6 * n + H, T), 1), acc)

        send_w[which, rims] = lax.fori_loop(0, 18, one, jnp.zeros((LEV, T), F32))

    in_west = ix <= half + 1
    in_east = ix >= half - 1
    pl.when(in_west)(lambda: share(WEST))
    pl.when(in_east)(lambda: share(EAST))

    def window_copy(which, part, x):
        span = (pl.ds(0, 4) if which else pl.ds(15, 4)) if part else pl.ds(0, 19)
        return rcopy(
            send_w.at[which, span], recv_w.at[which, span], win_ss.at[which], win_rs.at[which], x, iy
        )

    def window_pass(which, part, x, receives):
        if receives:
            span = (0, 4) if which and part else (15, 19) if part else (0, 19)
            window_copy(which, part, lax.rem(ix + 1, X)).wait_recv()

            def add(n, carry):
                send_w[which, n] = send_w[which, n] + recv_w[which, n]
                return carry

            lax.fori_loop(span[0], span[1], add, 0)

    pl.when(ix == half + 1)(lambda: window_copy(WEST, True, ix - 1).start())
    pl.when(ix == half - 1)(lambda: window_copy(EAST, True, ix + 1).start())
    late_down = (ix == half + 1) & (ix != 1)
    pl.when(late_down)(lambda: halo_copy(True).start())

    def take_rows(src, dx, first_row, count, at):
        def one(n, carry):
            k, r = n // count, lax.rem(n, count)
            sa[k, at + r, :, 0:C] = src[k, r]
            sa[k, at + r, :, C:W] = unpack(dx, H * (k * N + first_row + r))
            return carry

        lax.fori_loop(0, 3 * count, one, 0)

    take_rows(nest, 0, 0, N, H)

    @pl.when(ix == half)
    def _():
        window_pass(WEST, True, None, True)
        pl.when(ix > 0)(lambda: window_copy(WEST, False, ix - 1).start())
        pl.when(ix > 1)(lambda: halo_copy(True).start())
        window_pass(EAST, True, None, True)
        pl.when(ix < X - 1)(lambda: window_copy(EAST, False, ix + 1).start())

    if half > 1:

        @pl.when((ix > 0) & (ix < half))
        def _():
            window_pass(WEST, False, None, True)
            window_copy(WEST, False, ix - 1).start()
            pl.when(ix > 1)(lambda: halo_copy(True).start())

        @pl.when((ix > half) & (ix < X - 1))
        def _():
            window_pass(EAST, False, None, True)
            window_copy(EAST, False, ix + 1).start()

    cE, cW, cN, cS = range(4)

    def step(src, r, width):
        wide = width // T

        def cf(i):
            return jnp.concatenate([coef[i]] * wide, axis=1)

        def nb(k):
            x = src[k, r]
            return x, pltpu.roll(x, width - 1, 1), pltpu.roll(x, 1, 1)

        u, un, us = nb(0)
        v, vn, vs = nb(1)
        p, pn, ps = nb(2)

        def adv(k, x, xn, xs):
            return (
                0.5 * x + cf(cE) * src[k, r + 1] + cf(cW) * src[k, r - 1] + cf(cN) * xn + cf(cS) * xs
            )

        fu = adv(0, u, un, us) - 0.3 * (src[2, r + 1] - src[2, r - 1])
        fv = adv(1, v, vn, vs) - 0.3 * (pn - ps)
        fp = adv(2, p, pn, ps) - 0.3 * (src[0, r + 1] - src[0, r - 1] + (vn - vs))
        deep = mixer.shape[0]
        outs = []
        for f in (fu, fv, fp):
            full = f
            if deep > LEV:
                full = jnp.concatenate([f, jnp.zeros((deep - LEV, width), F32)], axis=0)
            hi, lo = split(full)
            stacked = jnp.concatenate([hi, hi, lo], axis=0)
            mixed = jnp.dot(mixer[...], stacked, preferred_element_type=F32)
            outs.append(f + mixed[:LEV])
        return outs

    @pl.when(ix > 0)
    def _():
        arrived(phb.at[0], ph_rs.at[0])

    @pl.when(ix < X - 1)
    def _():
        arrived(phb.at[1], ph_rs.at[1])

    pl.when(ix == 0)(lambda: phb.__setitem__(0, jnp.zeros((3, LEV, T), F32)))
    pl.when(ix == X - 1)(lambda: phb.__setitem__(1, jnp.zeros((3, LEV, T), F32)))
    for k in range(3):
        px[k, 0, :, 0:T] = phb[0, k]
        px[k, R + 1, :, 0:T] = phb[1, k]
        px[k, 0, :, T : 2 * T] = jnp.zeros((LEV, T), F32)
        px[k, R + 1, :, T : 2 * T] = jnp.zeros((LEV, T), F32)

    def parent_row(r, carry):
        for k, f in enumerate(step(px, r + 1, 2 * T)):
            parent_out[k, r] = f[:, 0:T]
        return carry

    lax.fori_loop(0, R, parent_row, 0)

    def masked(f, width):
        at = lanes((1, T))
        off_left = ((at >= T // 2) & (iy == 0)) | ((at < T // 2) & (iy == Y - 1))
        tail = jnp.where(off_left, 0.0, f[:, width - T : width])
        return jnp.concatenate([f[:, 0 : width - T], tail], axis=1)

    def run(src, dst, lo, hi):
        def one(r, carry):
            for k, f in enumerate(step(src, r, W)):
                dst[k, r] = masked(f, W)
            return carry

        lax.fori_loop(lo, hi, one, 0)

    def run_out(lo, hi):
        def one(r, carry):
            for k, f in enumerate(step(sb_last, r, W)):
                nest_out[k, r - H] = f[:, 0:C]
            return carry

        lax.fori_loop(lo, hi, one, 0)

    sb_last = sa
    top = N + 2 * H
    at_w, at_e = H + 3, H + N - 4
    lo1 = jnp.where(is_west, at_w + 1, 1)
    hi1 = jnp.where(is_east, at_e, top - 1)
    lo2 = jnp.where(is_west, at_w + 2, 2)
    hi2 = jnp.where(is_east, at_e - 1, top - 2)
    run(sa, sb, jnp.maximum(lo1, H + 1), jnp.minimum(hi1, H + N - 1))

    outer = is_west | is_east
    e = jnp.where(is_west, 0, 1)
    b_adj = jnp.where(is_west, 3, 0)

    def wt_copy(side):
        src = wx.at[:, :, C - T : C] if side else wx.at[:, :, 0:T]
        return rcopy(src, wrb.at[1 - side], wt_ss.at[side], wt_rs.at[1 - side], ix, col_partner(side))

    @pl.when(outer)
    def _():
        for row in range(4):
            for dc in range(3):
                acc = jnp.zeros((4, C), F32)
                for n in range(4):
                    hit = (d_rows[n, e] == row) & (d_cols[n, e] == dc - 1)
                    acc = acc + jnp.where(hit, d_wts[n, e], 0.0)
                wx[row * 3 + dc] = acc
        for side in (0, 1):
            pl.when(has_col[side])(lambda: wt_copy(side).start())
            pl.when(jnp.logical_not(has_col[side]))(
                lambda: wrb.__setitem__(side, jnp.zeros((12, 4, T), F32))
            )

    @pl.when(ix > 0)
    def _():
        pack_wait(-1)
        arrived(hl, halo_rs.at[0])
        take_rows(hl, -1, N - H, H, 0)

    @pl.when(ix < X - 1)
    def _():
        pack_wait(1)
        arrived(hh, halo_rs.at[1])
        take_rows(hh, 1, 0, H, H + N)

    run(sa, sb, lo1, jnp.minimum(hi1, H + 1))
    run(sa, sb, jnp.maximum(lo1, H + N - 1), hi1)
    run(sb, sa, lo2, hi2)

    def edge_work(which):
        base = 1 if which else 0
        rims = 0 if which else 18
        window_pass(which, False, None, True)

        def lay(n, carry):
            t, k = n // 3, lax.rem(n, 3)
            zb[k, t, :, 0:T] = send_w[which, base + n]
            tail = pltpu.roll(send_w[which, rims], lax.rem(2 * T - 6 * n - H, T), 1)
            zb[k, t, :, T : 2 * T] = jnp.where(rim_spot, tail, 0.0)
            return carry

        lax.fori_loop(0, 18, lay, 0)

    pl.when(is_west)(lambda: edge_work(WEST))
    pl.when(is_east)(lambda: edge_work(EAST))

    @pl.when(outer)
    def _():
        def zone_row(r, carry):
            for k, f in enumerate(step(zb, r + 1, 2 * T)):
                zn[k, r] = masked(f, 2 * T)
            return carry

        lax.fori_loop(0, 4, zone_row, 0)
        for side in (0, 1):
            pl.when(has_col[side])(lambda: arrived(wrb.at[side], wt_rs.at[side]))
        at8 = lanes((8, T))
        for b in range(4):
            for i in range(12):
                left = jnp.broadcast_to(wrb[0, i, b : b + 1, :], (8, T))
                right = jnp.broadcast_to(wrb[1, i, b : b + 1, :], (8, T))
                wxb[i, b, :, 0:C] = jnp.broadcast_to(wx[i, b : b + 1, :], (8, C))
                wxb[i, b, :, C:W] = jnp.where(at8 < T // 2, right, left)

        y = lanes((2 * T, W))
        c = lanes((2 * T, W), 0)
        y = jnp.where(y < C + T // 2, y, y - W)
        c = jnp.where(c < T + T // 2, c, c - 2 * T)
        for dc in range(3):
            gap = y - 3 * (c - (dc - 1))
            hot = jnp.where((gap >= 0) & (gap <= 2), 1.0, 0.0).astype(BF16)

            def spread(k, carry):
                for time in range(2):
                    rows = zn[k] if time else zb[k, 1:5]
                    hi, lo = split(rows.reshape(4 * LEV, 2 * T))
                    got = jnp.dot(hi, hot, preferred_element_type=F32) + jnp.dot(
                        lo, hot, preferred_element_type=F32
                    )
                    grid[time, k, dc] = got.reshape(4, LEV, W)
                return carry

            lax.fori_loop(0, 3, spread, 0)

        def bound(time, k, b):
            acc = jnp.zeros((LEV, W), F32)
            for row in range(4):
                for dc in range(3):
                    w = jnp.concatenate([wxb[row * 3 + dc, b]] * (LEV // 8), axis=0)
                    acc = acc + w * grid[time, k, dc, row]
            return acc

        def each(n, carry):
            k, b = n // 4, lax.rem(n, 4)
            got = bound(1, k, b)
            b1[b, k] = got
            nest_out[k, jnp.where(is_west, 0, N - 4) + b] = got[:, 0:C]
            return carry

        lax.fori_loop(0, 12, each, 0)

        def each0(k, carry):
            b0[k] = bound(0, k, b_adj)
            return carry

        lax.fori_loop(0, 3, each0, 0)

        ra = jnp.where(is_west, at_w, at_e)
        r2 = jnp.where(is_west, at_w + 1, at_e - 1)
        for k in range(3):
            sb[k, ra] = (1.0 - 1.0 / 3.0) * b0[k] + (1.0 / 3.0) * b1[b_adj, k]
        run(sb, sa, r2, r2 + 1)
        for k in range(3):
            sa[k, ra] = (1.0 - 2.0 / 3.0) * b0[k] + (2.0 / 3.0) * b1[b_adj, k]

    run_out(jnp.where(is_west, at_w + 1, H), jnp.where(is_east, at_e, H + N))

    per = N // 3
    sums = []
    for g in range(per):
        for k in range(3):
            sums.append(nest_out[k, 3 * g] + nest_out[k, 3 * g + 1] + nest_out[k, 3 * g + 2])
    hi, lo = split(jnp.concatenate(sums, axis=0))
    gap = lanes((C, T), 0) - 3 * lanes((C, T))
    pool = jnp.where((gap >= 0) & (gap <= 2), 1.0, 0.0).astype(BF16)
    mean = jnp.dot(hi, pool, preferred_element_type=F32) + jnp.dot(lo, pool, preferred_element_type=F32)
    co[...] = (mean * (1.0 / 9.0)).reshape(per, 3, LEV, T)

    def co_copy(g, m):
        return rcopy(co.at[g], cb.at[per * ix + g], co_ss.at[m, g], co_rs.at[per * ix + g], 1 + ix // 2 + m, iy)

    def co_each(action):
        for m in range(half):
            for g in range(per):
                inner = jnp.logical_not(is_west) if g == 0 else jnp.logical_not(is_east)
                pl.when(inner & (1 + ix // 2 + m != ix))(lambda: action(co_copy(g, m)))

    co_each(lambda copy: copy.start())

    def put(src, g):
        for i in range(R):
            hit = a0 + g == R * ix + i
            for k in range(3):
                parent_out[k, i] = jnp.where(hit, src[k], parent_out[k, i])

    def feed(g, carry):
        j = g // per
        reach = (1 + j // 2 <= ix) & (ix <= half + j // 2)

        @pl.when(reach & (j != ix))
        def _():
            arrived(cb.at[g], co_rs.at[g])
            put(cb.at[g], g)

        @pl.when(reach & (j == ix))
        def _():
            put(co.at[lax.rem(g, per)], g)

        return carry

    lax.fori_loop(1, per * X - 1, feed, 0)

    for dx in (0, -1, 1):
        for side in (0, 1):
            pl.when(has_col[side] & row_ok(dx))(lambda: pack_copy(side, dx).wait_send())
    pl.when(ix > 0)(lambda: ph_copy(True).wait_send())
    pl.when(ix < X - 1)(lambda: ph_copy(False).wait_send())
    pl.when(ix > 0)(lambda: halo_copy(True).wait_send())
    pl.when(ix < X - 1)(lambda: halo_copy(False).wait_send())
    pl.when(ix == half + 1)(lambda: window_copy(WEST, True, ix - 1).wait_send())
    pl.when((ix > 0) & (ix <= half))(lambda: window_copy(WEST, False, ix - 1).wait_send())
    pl.when(ix == half - 1)(lambda: window_copy(EAST, True, ix + 1).wait_send())
    pl.when((ix >= half) & (ix < X - 1))(lambda: window_copy(EAST, False, ix + 1).wait_send())
    for side in (0, 1):
        pl.when(outer & has_col[side])(lambda: wt_copy(side).wait_send())
    co_each(lambda copy: copy.wait_send())


def shards(parent, nest, nest_anchor, donor_rows, donor_cols, donor_weights, wind_x, wind_y, column_mix):
    X = lax.axis_size("gx")
    CY = lax.axis_size("gz")
    Y = lax.axis_size("gy") * CY
    LEV, R = parent.shape[1], parent.shape[2]
    N, C = nest.shape[2], nest.shape[3]
    W = C + T
    top = N + 2 * H
    per = N // 3
    deep = -(-LEV // 16) * 16
    hi = lax.reduce_precision(column_mix, 8, 7)
    hi, lo = (jnp.pad(x, ((0, deep - LEV), (0, deep - LEV))) for x in (hi, column_mix - hi))
    mixer = jnp.concatenate([hi, lo, hi], axis=1).astype(BF16)
    wx, wy = 0.5 * wind_x, 0.5 * wind_y
    coef = jnp.stack([0.125 - wx, 0.125 + wx, 0.125 - wy, 0.125 + wy])
    coef = jnp.broadcast_to(coef[:, :, None], (4, LEV, T))
    vmem = pl.BlockSpec(memory_space=pltpu.VMEM)
    smem = pl.BlockSpec(memory_space=pltpu.SMEM)
    V = lambda *s: pltpu.VMEM(s, F32)
    D = lambda *s: pltpu.SemaphoreType.DMA(s)
    outs = pl.pallas_call(
        functools.partial(kernel, X, Y, CY),
        out_shape=(
            jax.ShapeDtypeStruct((3, R, LEV, T), F32),
            jax.ShapeDtypeStruct((3, N, LEV, C), F32),
        ),
        in_specs=[vmem, vmem, smem, vmem, vmem, vmem, vmem, vmem],
        out_specs=(vmem, vmem),
        scratch_shapes=[
            V(2, LEV, T),
            V(3, 2, LEV, T),
            V(2, 3, LEV, T),
            V(3, H, LEV, C),
            V(3, H, LEV, C),
            V(3, R + 2, LEV, 2 * T),
            V(3, top, LEV, W),
            V(3, top, LEV, W),
            V(2, 19, LEV, T),
            V(2, 19, LEV, T),
            V(3, 6, LEV, 2 * T),
            V(3, 4, LEV, 2 * T),
            V(2, 3, 3, 4, LEV, W),
            V(12, 4, C),
            V(2, 12, 4, T),
            V(12, 4, 8, W),
            V(3, LEV, W),
            V(4, 3, LEV, W),
            V(per, 3, LEV, T),
            V(per * X, 3, LEV, T),
            D(3, 2), D(3, 2), D(2), D(2), D(2), D(2), D(2), D(2), D(2), D(2), D(X // 2, per), D(per * X),
        ],
        compiler_params=pltpu.CompilerParams(
            collective_id=0, has_side_effects=True, vmem_limit_bytes=48 * 1024 * 1024
        ),
        cost_estimate=pl.CostEstimate(flops=200_000_000, bytes_accessed=6_000_000, transcendentals=0),
    )(
        parent.transpose(0, 2, 1, 3),
        nest.transpose(0, 2, 1, 3),
        nest_anchor,
        donor_rows,
        donor_cols,
        donor_weights,
        coef,
        mixer,
    )
    return tuple(x.transpose(0, 2, 1, 3) for x in outs)


def solution(mesh):
    grids = P("member", None, "gx", ("gy", "gz"))
    donors = P("member", None, None, ("gy", "gz"))
    return jax.shard_map(
        shards,
        mesh=mesh,
        in_specs=(grids, grids, P("member"), donors, donors, donors, P(), P(), P()),
        out_specs=(grids, grids),
        check_vma=False,
    )
```

time: 411 us -> 56.9 us (0.14); the launches traced: 406 us -> 56.4 us
  local copies, waits for them, and re-layouts: 178 us -> 6.43 us
  other arithmetic: 101 us -> 2.24 us
  starting transfers between devices: 49.3 us -> 0 us
  Pallas kernels: 0 us -> 46.4 us
  blocking collectives: 44.4 us -> 0 us
  waiting for transfers between devices: 22.8 us -> 0 us
  matrix products: 8.64 us -> 0 us
    gather x7 -> x0, local copies, waits for them, and re-layouts: 140 us -> none  [the longest x1 128 us: sample_zone(): picked = jnp.take(flattened, flat_index, axis=-1)]
    reduce_sum x3 -> x0, other arithmetic: 67.3 us -> none  [the longest x1 63.1 us: sample_zone(): return jnp.sum(picked * donor_weights, axis=-4)]
    ppermute x18 -> x0, starting transfers between devices: 49.3 us -> none  [the longest x9 25.4 us: padded_2(): lax.ppermute(lax.slice_in_dim(block, 0, width, axis=dim), axis, backward)]
    pallas_call x0 -> x1, Pallas kernels: none -> 46.4 us  [shards(): pl.pallas_call(functools.partial(kernel, X, Y, CY), out_shape=(jax.ShapeD...]
    all_gather x2 -> x0, blocking collectives: 44.4 us -> none  [the longest x1 30.5 us: shards(): piece = lax.all_gather(rimmed, 'gx', axis=2, tiled=True)]
    ppermute x18 -> x0, waiting for transfers between devices: 22.8 us -> none  [the longest x9 18.6 us: padded_2(): lax.ppermute(lax.slice_in_dim(block, block.shape[dim] - width, None, axis...]
    reshape x2 -> x0, local copies, waits for them, and re-layouts: 12.2 us -> none  [the longest x1 6.43 us: shards(): nest_state.reshape(3, levels, nest_rows // 3, 3, nest_cols // 3, 3)]
    reduce_sum x2 -> x0, local copies, waits for them, and re-layouts: 11.6 us -> none  [the longest x1 11.5 us: sample_zone(): return jnp.sum(picked * donor_weights, axis=-4)]
  transfers between devices with their start and end apart: 18 -> 0, of which waited for: 10 -> 0; matrix products, arithmetic and copies ran while one was open for 61% -> 0% of each run, Pallas kernels for 0% -> 0%
where the time goes in v1:
time: 56.9 us; the launch traced here: 56.4 us
  Pallas kernels  46.4 us (82%)
  local copies, waits for them, and re-layouts  6.43 us (11%)
  other arithmetic  2.24 us (4%)
  between operations  1.31 us (2%)
    pallas_call x1, Pallas kernels, shards(): pl.pallas_call(functools.partial(kernel, X, Y, CY), out_shape=(jax.ShapeD...  46.4 us
    unnamed x11, local copies, waits for them, and re-layouts  6.35 us

profile of v1, /device:TPU:18, one launch (start us, length us, event | category | flops | bytes accessed | tf_op | source)
XLA Modules:
  0.0 56.4 jit_solution(15179938749004859577)
XLA Ops:
  1.3 0.7 %subtract_bitcast_fusion = (f32[1,40]{1,0:T(1,128)S(1)}, f32[1,40]{1,0:T(1,128)S(1)}, f32[1,40]{1,0:T(1,128)S(1)}, f32[1,40]{1,0:T(1,128)S(1)}) fusion(f32[40]{0:T(128)} %param.16, f32[40]{0:T(128)} %param.15), kind=kLoop, calls=%fused_computation.11 | loop fusion | flops 240 | bytes 960 | tf_op jit(solution)/shard_map/stack | solution.py:528
  2.0 0.7 %subtract_convert_fusion = bf16[40,40]{1,0:T(8,128)(2,1)S(1)} fusion(f32[40,40]{1,0:T(8,128)} %param.17), kind=kLoop, calls=%fused_computation.8 | loop fusion | flops 4800 | bytes 9600 | tf_op jit(solution)/shard_map/convert.3
  2.7 0.7 %reduce_precision.3 = bf16[40,40]{1,0:T(8,128)(2,1)S(1)} reduce-precision(f32[40,40]{1,0:T(8,128)} %param.17), exponent_bits=8, mantissa_bits=7 | non-fusion elementwise | flops 1600 | bytes 9600 | tf_op jit(solution)/shard_map/reduce_precision | solution.py:524
  3.4 0.1 fusion.3.mixer
  3.5 0.1 broadcast_in_dim.2.coef
  3.6 1.0 %copy.14 = f32[3,40,4,128]{3,1,2,0:T(8,128)S(1)} copy(f32[3,40,4,128]{3,2,1,0:T(4,128)} %param.9) | data formatting | bytes 491520 | tf_op args[0]
  4.6 0.0 copy-start
  4.6 1.2 %copy-done = f32[3,40,6,384]{3,1,2,0:T(8,128)S(1)} copy-done((f32[3,40,6,384]{3,1,2,0:T(8,128)S(1)}, f32[3,40,6,384]{3,1,2,0:T(8,128)}, u32[]{:S(2)}) %copy-start) | copy-done | bytes 1105944
  5.8 0.0 copy-start.1
  5.8 0.8 %copy-done.1 = s32[4,2,4,384]{3,2,1,0:T(4,128)S(1)} copy-done((s32[4,2,4,384]{3,2,1,0:T(4,128)S(1)}, s32[4,2,4,384]{3,2,1,0:T(4,128)}, u32[]{:S(2)}) %copy-start.1) | copy-done | bytes 49176
  6.6 0.0 copy-start.2
  6.6 0.8 %copy-done.2 = s32[4,2,4,384]{3,2,1,0:T(4,128)S(1)} copy-done((s32[4,2,4,384]{3,2,1,0:T(4,128)S(1)}, s32[4,2,4,384]{3,2,1,0:T(4,128)}, u32[]{:S(2)}) %copy-start.2) | copy-done | bytes 49176
  7.4 0.0 copy-start.3
  7.4 0.8 %copy-done.3 = f32[4,2,4,384]{3,2,1,0:T(4,128)S(1)} copy-done((f32[4,2,4,384]{3,2,1,0:T(4,128)S(1)}, f32[4,2,4,384]{3,2,1,0:T(4,128)}, u32[]{:S(2)}) %copy-start.3) | copy-done | bytes 49176
  8.2 46.4 %shard_map.104 = (f32[3,4,40,128]{3,2,1,0:T(8,128)S(1)}, f32[3,6,40,384]{3,2,1,0:T(8,128)S(1)}) custom-call(f32[3,4,40,128]{3,2,1,0:T(8,128)S(1)} %bitcast.16, f32[3,6,40,384]{3,2,1,0:T(8,128)S(1)} %bitcast.14, s32[1]{0:T(128)S(6)} %copy.16.anchor, s32[4,2,4,384]{3,2,1,0:T(4,128)S(1)} %copy-done.1, s32[4,2,4,384]{3,2,1,0:T(4,128)S(1)} %copy-done.2, ...), custom_call_target="tpu_custom_call" | custom-call | flops 200000000 | bytes 6000000 | tf_op jit(solution)/shard_map/pallas_call | solution.py:534
  54.7 0.8 %copy.12 = f32[3,40,4,128]{3,2,1,0:T(4,128)} copy(f32[3,40,4,128]{3,1,2,0:T(8,128)S(1)} %bitcast.17) | data formatting | bytes 491520
  55.4 1.0 %copy.17 = f32[3,40,6,384]{3,1,2,0:T(8,128)} copy(f32[3,40,6,384]{3,1,2,0:T(8,128)S(1)} %bitcast.15) | data formatting | bytes 2211840
  (2 shorter events, 0.0 us)
Async XLA Ops:
  4.6 1.2 %copy-start = (f32[3,40,6,384]{3,1,2,0:T(8,128)S(1)}, f32[3,40,6,384]{3,1,2,0:T(8,128)}, u32[]{:S(2)}) copy-start(f32[3,40,6,384]{3,1,2,0:T(8,128)} %param.10) | copy-start | bytes 3317764
  5.8 0.8 %copy-start.1 = (s32[4,2,4,384]{3,2,1,0:T(4,128)S(1)}, s32[4,2,4,384]{3,2,1,0:T(4,128)}, u32[]{:S(2)}) copy-start(s32[4,2,4,384]{3,2,1,0:T(4,128)} %d_rows.1) | copy-start | bytes 147460
  6.6 0.8 %copy-start.2 = (s32[4,2,4,384]{3,2,1,0:T(4,128)S(1)}, s32[4,2,4,384]{3,2,1,0:T(4,128)}, u32[]{:S(2)}) copy-start(s32[4,2,4,384]{3,2,1,0:T(4,128)} %d_cols.1) | copy-start | bytes 147460
  7.4 0.8 %copy-start.3 = (f32[4,2,4,384]{3,2,1,0:T(4,128)S(1)}, f32[4,2,4,384]{3,2,1,0:T(4,128)}, u32[]{:S(2)}) copy-start(f32[4,2,4,384]{3,2,1,0:T(4,128)} %d_wts.1) | copy-start | bytes 147460

commit v2 on v1

--- a/solution.py
+++ b/solution.py
@@ -27,11 +27,19 @@
 
 def kernel(
     X, Y, CY,
-    parent, nest, anchor, d_rows, d_cols, d_wts, coef, mixer,
+    parent_in, nest_in, anchor, rows_in, cols_in, wts_in, wind_x_in, wind_y_in, mix_in,
     parent_out, nest_out,
-    edge, pb, phb, hl, hh, px, sa, sb, send_w, recv_w, zb, zn, grid, wx, wrb, wxb, b0, b1, co, cb,
+    raw, nest, d_rows, d_cols, d_wts, wind_x, wind_y, mix, parent, coef, mixer, packed, hot,
+    edge, pb, phb, hl, hh, px, sa, sb, send_w, recv_w, zb, zn, grid, wx, wrb, wxb, b0, b1, co, cb, load_s,
     pack_ss, pack_rs, ph_ss, ph_rs, halo_ss, halo_rs, win_ss, win_rs, wt_ss, wt_rs, co_ss, co_rs,
 ):
+    pairs = (
+        (nest_in, nest), (parent_in, raw), (wind_x_in, wind_x), (wind_y_in, wind_y), (mix_in, mix),
+        (rows_in, d_rows), (cols_in, d_cols), (wts_in, d_wts),
+    )
+    loads = [pltpu.make_async_copy(a, b, load_s.at[i]) for i, (a, b) in enumerate(pairs)]
+    for load in loads:
+        load.start()
     R = parent.shape[1]
     N = nest.shape[1]
     LEV = nest.shape[2]
@@ -54,7 +62,7 @@
         )
 
     def arrived(ref, rs):
-        rcopy(ref, ref, halo_ss.at[0], rs, lax.rem(ix + 1, X), iy).wait_recv()
+        rcopy(ref, ref, halo_ss.at[0, 0], rs, lax.rem(ix + 1, X), iy).wait_recv()
 
     def col_partner(side):
         return iy + (1 if side else -1)
@@ -78,6 +86,11 @@
                 )
 
     lane = lanes((LEV, T))
+    loads[0].wait()
+    loads[1].wait()
+    for k in range(3):
+        for r in range(R):
+            parent[k, r] = raw[k, :, r, :]
     edge[...] = jnp.zeros_like(edge)
 
     def pack_nest(n, carry):
@@ -112,10 +125,15 @@
             return rcopy(parent.at[:, 0], phb.at[1], ph_ss.at[1], ph_rs.at[1], ix - 1, iy)
         return rcopy(parent.at[:, R - 1], phb.at[0], ph_ss.at[0], ph_rs.at[0], ix + 1, iy)
 
-    def halo_copy(down):
+    def halo_copy(down, j):
         if down:
-            return rcopy(nest.at[:, 0:H], hh, halo_ss.at[1], halo_rs.at[1], ix - 1, iy)
-        return rcopy(nest.at[:, N - H : N], hl, halo_ss.at[0], halo_rs.at[0], ix + 1, iy)
+            return rcopy(nest.at[:, j], hh.at[:, j], halo_ss.at[1, j], halo_rs.at[1, j], ix - 1, iy)
+        i = H - 1 - j
+        return rcopy(nest.at[:, N - 1 - j], hl.at[:, i], halo_ss.at[0, j], halo_rs.at[0, j], ix + 1, iy)
+
+    def halo_send(down, rows):
+        for j in rows:
+            halo_copy(down, j).start()
 
     for dx in (0, -1, 1):
         for side in (0, 1):
@@ -126,9 +144,10 @@
             )
     pl.when(ix > 0)(lambda: ph_copy(True).start())
     pl.when(ix < X - 1)(lambda: ph_copy(False).start())
-    early_down = (ix == 1) | (ix > half + 1)
-    pl.when(early_down)(lambda: halo_copy(True).start())
-    pl.when(ix < X - 1)(lambda: halo_copy(False).start())
+    pl.when(ix > 0)(lambda: halo_send(True, (0,)))
+    pl.when(ix < X - 1)(lambda: halo_send(False, (0,)))
+    pl.when(ix > half)(lambda: halo_send(True, (1, 2)))
+    pl.when(ix < half)(lambda: halo_send(False, (1, 2)))
 
     def pack_wait(dx):
         for side in (0, 1):
@@ -179,60 +198,98 @@
     pl.when(in_west)(lambda: share(WEST))
     pl.when(in_east)(lambda: share(EAST))
 
-    def window_copy(which, part, x):
-        span = (pl.ds(0, 4) if which else pl.ds(15, 4)) if part else pl.ds(0, 19)
+    spans = (((0, 6), (6, 12), (12, 15), (15, 19)), ((13, 19), (7, 13), (4, 7), (0, 4)))
+
+    def window_copy(which, c, x):
+        lo, hi = spans[which][c]
+        span = pl.ds(lo, hi - lo)
         return rcopy(
-            send_w.at[which, span], recv_w.at[which, span], win_ss.at[which], win_rs.at[which], x, iy
+            send_w.at[which, span], recv_w.at[which, span], win_ss.at[which, c], win_rs.at[which, c], x, iy
         )
 
-    def window_pass(which, part, x, receives):
-        if receives:
-            span = (0, 4) if which and part else (15, 19) if part else (0, 19)
-            window_copy(which, part, lax.rem(ix + 1, X)).wait_recv()
-
-            def add(n, carry):
-                send_w[which, n] = send_w[which, n] + recv_w[which, n]
-                return carry
-
-            lax.fori_loop(span[0], span[1], add, 0)
-
-    pl.when(ix == half + 1)(lambda: window_copy(WEST, True, ix - 1).start())
-    pl.when(ix == half - 1)(lambda: window_copy(EAST, True, ix + 1).start())
-    late_down = (ix == half + 1) & (ix != 1)
-    pl.when(late_down)(lambda: halo_copy(True).start())
-
-    def take_rows(src, dx, first_row, count, at):
+    def window_add(which, c):
+        window_copy(which, c, lax.rem(ix + 1, X)).wait_recv()
+
+        def add(n, carry):
+            send_w[which, n] = send_w[which, n] + recv_w[which, n]
+            return carry
+
+        lax.fori_loop(spans[which][c][0], spans[which][c][1], add, 0)
+
+    pl.when(ix == half + 1)(lambda: window_copy(WEST, 3, ix - 1).start())
+    pl.when(ix == half - 1)(lambda: window_copy(EAST, 3, ix + 1).start())
+
+    @pl.when(ix == half)
+    def _():
+        for c in range(3):
+            window_copy(WEST, c, ix - 1).start()
+            if half < X - 1:
+                window_copy(EAST, c, ix + 1).start()
+
+    def take_rows(src, dx, first_row, count, at, only=None):
         def one(n, carry):
-            k, r = n // count, lax.rem(n, count)
+            k, r = (n // count, n % count) if only is not None else (n // count, lax.rem(n, count))
             sa[k, at + r, :, 0:C] = src[k, r]
             sa[k, at + r, :, C:W] = unpack(dx, H * (k * N + first_row + r))
             return carry
 
-        lax.fori_loop(0, 3 * count, one, 0)
+        if only is None:
+            lax.fori_loop(0, 3 * count, one, 0)
+        else:
+            for k in range(3):
+                one(k * count + only, 0)
 
     take_rows(nest, 0, 0, N, H)
 
     @pl.when(ix == half)
     def _():
-        window_pass(WEST, True, None, True)
-        pl.when(ix > 0)(lambda: window_copy(WEST, False, ix - 1).start())
-        pl.when(ix > 1)(lambda: halo_copy(True).start())
-        window_pass(EAST, True, None, True)
-        pl.when(ix < X - 1)(lambda: window_copy(EAST, False, ix + 1).start())
+        window_add(WEST, 3)
+        window_copy(WEST, 3, ix - 1).start()
+        window_add(EAST, 3)
+        if half < X - 1:
+            window_copy(EAST, 3, ix + 1).start()
 
     if half > 1:
 
         @pl.when((ix > 0) & (ix < half))
         def _():
-            window_pass(WEST, False, None, True)
-            window_copy(WEST, False, ix - 1).start()
-            pl.when(ix > 1)(lambda: halo_copy(True).start())
+            for c in range(4):
+                window_add(WEST, c)
+                window_copy(WEST, c, ix - 1).start()
+
+    if half + 1 < X - 1:
 
         @pl.when((ix > half) & (ix < X - 1))
         def _():
-            window_pass(EAST, False, None, True)
-            window_copy(EAST, False, ix + 1).start()
-
+            for c in range(4):
+                window_add(EAST, c)
+                window_copy(EAST, c, ix + 1).start()
+
+    pl.when((ix > 0) & (ix <= half))(lambda: halo_send(True, (1, 2)))
+    pl.when((ix < X - 1) & (ix >= half))(lambda: halo_send(False, (1, 2)))
+
+    for load in loads[2:5]:
+        load.wait()
+    diagonal = lanes((LEV, LEV)) == lanes((LEV, LEV), 0)
+
+    def column(ref):
+        w = jnp.where(diagonal, jnp.broadcast_to(ref[...], (LEV, LEV)), 0.0)
+        return jnp.broadcast_to(0.5 * jnp.sum(w, axis=1, keepdims=True), (LEV, T))
+
+    wind = column(wind_x)
+    coef[0] = 0.125 - wind
+    coef[1] = 0.125 + wind
+    wind = column(wind_y)
+    coef[2] = 0.125 - wind
+    coef[3] = 0.125 + wind
+    mixer[...] = jnp.zeros_like(mixer)
+    for i in range(3):
+        whole = mix[...]
+        top_part = whole.astype(BF16).astype(F32)
+        mixer[i, 0:LEV, 0:LEV] = whole - top_part if i == 1 else top_part
+    DEEP = mixer.shape[2]
+    placed = mixer[0] + pltpu.roll(mixer[1], LEV, 1) + pltpu.roll(mixer[2], 2 * LEV, 1)
+    packed[...] = placed.astype(BF16)
     cE, cW, cN, cS = range(4)
 
     def step(src, r, width):
@@ -257,15 +314,13 @@
         fu = adv(0, u, un, us) - 0.3 * (src[2, r + 1] - src[2, r - 1])
         fv = adv(1, v, vn, vs) - 0.3 * (pn - ps)
         fp = adv(2, p, pn, ps) - 0.3 * (src[0, r + 1] - src[0, r - 1] + (vn - vs))
-        deep = mixer.shape[0]
         outs = []
         for f in (fu, fv, fp):
-            full = f
-            if deep > LEV:
-                full = jnp.concatenate([f, jnp.zeros((deep - LEV, width), F32)], axis=0)
-            hi, lo = split(full)
-            stacked = jnp.concatenate([hi, hi, lo], axis=0)
-            mixed = jnp.dot(mixer[...], stacked, preferred_element_type=F32)
+            hi = f.astype(BF16).astype(F32)
+            stacked = jnp.concatenate([hi, hi, f - hi], axis=0)
+            if DEEP > 3 * LEV:
+                stacked = jnp.concatenate([stacked, jnp.zeros((DEEP - 3 * LEV, width), F32)], axis=0)
+            mixed = jnp.dot(packed[...], stacked.astype(BF16), preferred_element_type=F32)
             outs.append(f + mixed[:LEV])
         return outs
 
@@ -306,30 +361,29 @@
 
         lax.fori_loop(lo, hi, one, 0)
 
-    def run_out(lo, hi):
-        def one(r, carry):
-            for k, f in enumerate(step(sb_last, r, W)):
-                nest_out[k, r - H] = f[:, 0:C]
-            return carry
-
-        lax.fori_loop(lo, hi, one, 0)
-
-    sb_last = sa
+    def run_out(r):
+        for k, f in enumerate(step(sa, r, W)):
+            nest_out[k, r - H] = f[:, 0:C]
+
     top = N + 2 * H
     at_w, at_e = H + 3, H + N - 4
-    lo1 = jnp.where(is_west, at_w + 1, 1)
-    hi1 = jnp.where(is_east, at_e, top - 1)
-    lo2 = jnp.where(is_west, at_w + 2, 2)
-    hi2 = jnp.where(is_east, at_e - 1, top - 2)
-    run(sa, sb, jnp.maximum(lo1, H + 1), jnp.minimum(hi1, H + N - 1))
-
     outer = is_west | is_east
+    inner = jnp.logical_not(outer)
+    run(sa, sb, jnp.where(is_west, at_w + 1, H + 1), jnp.where(is_east, at_e, H + N - 1))
+
+    @pl.when(inner)
+    def _():
+        run(sb, sa, H + 2, H + N - 2)
+
     e = jnp.where(is_west, 0, 1)
     b_adj = jnp.where(is_west, 3, 0)
 
     def wt_copy(side):
         src = wx.at[:, :, C - T : C] if side else wx.at[:, :, 0:T]
         return rcopy(src, wrb.at[1 - side], wt_ss.at[side], wt_rs.at[1 - side], ix, col_partner(side))
+
+    for load in loads[5:]:
+        load.wait()
 
     @pl.when(outer)
     def _():
@@ -346,47 +400,39 @@
                 lambda: wrb.__setitem__(side, jnp.zeros((12, 4, T), F32))
             )
 
+    def take(j, low):
+        if low:
+            arrived(hl.at[:, H - 1 - j], halo_rs.at[0, j])
+            take_rows(hl, -1, N - H, H, 0, H - 1 - j)
+        else:
+            arrived(hh.at[:, j], halo_rs.at[1, j])
+            take_rows(hh, 1, 0, H, H + N, j)
+
+    def at(j, s, low):
+        return H - j + s - 1 if low else H + N - 1 + j - s + 1
+
+    def one_row(src, dst, r):
+        run(src, dst, r, r + 1)
+
+    def grow(j, low):
+        one_row(sa, sb, at(j, 1, low))
+        one_row(sb, sa, at(j, 2, low))
+        run_out(at(j, 3, low))
+
     @pl.when(ix > 0)
     def _():
         pack_wait(-1)
-        arrived(hl, halo_rs.at[0])
-        take_rows(hl, -1, N - H, H, 0)
+        take(0, True)
+        one_row(sa, sb, at(0, 1, True))
 
     @pl.when(ix < X - 1)
     def _():
         pack_wait(1)
-        arrived(hh, halo_rs.at[1])
-        take_rows(hh, 1, 0, H, H + N)
-
-    run(sa, sb, lo1, jnp.minimum(hi1, H + 1))
-    run(sa, sb, jnp.maximum(lo1, H + N - 1), hi1)
-    run(sb, sa, lo2, hi2)
-
-    def edge_work(which):
-        base = 1 if which else 0
-        rims = 0 if which else 18
-        window_pass(which, False, None, True)
-
-        def lay(n, carry):
-            t, k = n // 3, lax.rem(n, 3)
-            zb[k, t, :, 0:T] = send_w[which, base + n]
-            tail = pltpu.roll(send_w[which, rims], lax.rem(2 * T - 6 * n - H, T), 1)
-            zb[k, t, :, T : 2 * T] = jnp.where(rim_spot, tail, 0.0)
-            return carry
-
-        lax.fori_loop(0, 18, lay, 0)
-
-    pl.when(is_west)(lambda: edge_work(WEST))
-    pl.when(is_east)(lambda: edge_work(EAST))
+        take(0, False)
+        one_row(sa, sb, at(0, 1, False))
 
     @pl.when(outer)
     def _():
-        def zone_row(r, carry):
-            for k, f in enumerate(step(zb, r + 1, 2 * T)):
-                zn[k, r] = masked(f, 2 * T)
-            return carry
-
-        lax.fori_loop(0, 4, zone_row, 0)
         for side in (0, 1):
             pl.when(has_col[side])(lambda: arrived(wrb.at[side], wt_rs.at[side]))
         at8 = lanes((8, T))
@@ -403,14 +449,42 @@
         c = jnp.where(c < T + T // 2, c, c - 2 * T)
         for dc in range(3):
             gap = y - 3 * (c - (dc - 1))
-            hot = jnp.where((gap >= 0) & (gap <= 2), 1.0, 0.0).astype(BF16)
+            hot[dc] = jnp.where((gap >= 0) & (gap <= 2), 1.0, 0.0).astype(BF16)
+
+    def edge_work(which):
+        base = 1 if which else 0
+        rims = 0 if which else 18
+        for c in range(4):
+            window_add(which, c)
+
+        def lay(n, carry):
+            t, k = n // 3, lax.rem(n, 3)
+            zb[k, t, :, 0:T] = send_w[which, base + n]
+            tail = pltpu.roll(send_w[which, rims], lax.rem(2 * T - 6 * n - H, T), 1)
+            zb[k, t, :, T : 2 * T] = jnp.where(rim_spot, tail, 0.0)
+            return carry
+
+        lax.fori_loop(0, 18, lay, 0)
+
+    pl.when(is_west)(lambda: edge_work(WEST))
+    pl.when(is_east)(lambda: edge_work(EAST))
+
+    @pl.when(outer)
+    def _():
+        def zone_row(r, carry):
+            for k, f in enumerate(step(zb, r + 1, 2 * T)):
+                zn[k, r] = masked(f, 2 * T)
+            return carry
+
+        lax.fori_loop(0, 4, zone_row, 0)
+        for dc in range(3):
 
             def spread(k, carry):
                 for time in range(2):
                     rows = zn[k] if time else zb[k, 1:5]
                     hi, lo = split(rows.reshape(4 * LEV, 2 * T))
-                    got = jnp.dot(hi, hot, preferred_element_type=F32) + jnp.dot(
-                        lo, hot, preferred_element_type=F32
+                    got = jnp.dot(hi, hot[dc], preferred_element_type=F32) + jnp.dot(
+                        lo, hot[dc], preferred_element_type=F32
                     )
                     grid[time, k, dc] = got.reshape(4, LEV, W)
                 return carry
@@ -441,14 +515,27 @@
         lax.fori_loop(0, 3, each0, 0)
 
         ra = jnp.where(is_west, at_w, at_e)
-        r2 = jnp.where(is_west, at_w + 1, at_e - 1)
         for k in range(3):
             sb[k, ra] = (1.0 - 1.0 / 3.0) * b0[k] + (1.0 / 3.0) * b1[b_adj, k]
-        run(sb, sa, r2, r2 + 1)
-        for k in range(3):
             sa[k, ra] = (1.0 - 2.0 / 3.0) * b0[k] + (2.0 / 3.0) * b1[b_adj, k]
 
-    run_out(jnp.where(is_west, at_w + 1, H), jnp.where(is_east, at_e, H + N))
+    @pl.when(ix > 0)
+    def _():
+        one_row(sb, sa, at(0, 2, True))
+        pl.when(inner)(lambda: run_out(at(0, 3, True)))
+
+    @pl.when(ix < X - 1)
+    def _():
+        one_row(sb, sa, at(0, 2, False))
+        pl.when(inner)(lambda: run_out(at(0, 3, False)))
+
+    for low in (True, False):
+
+        @pl.when(ix > 0 if low else ix < X - 1)
+        def _():
+            for j in (1, 2):
+                take(j, low)
+                grow(j, low)
 
     per = N // 3
     sums = []
@@ -500,12 +587,14 @@
             pl.when(has_col[side] & row_ok(dx))(lambda: pack_copy(side, dx).wait_send())
     pl.when(ix > 0)(lambda: ph_copy(True).wait_send())
     pl.when(ix < X - 1)(lambda: ph_copy(False).wait_send())
-    pl.when(ix > 0)(lambda: halo_copy(True).wait_send())
-    pl.when(ix < X - 1)(lambda: halo_copy(False).wait_send())
-    pl.when(ix == half + 1)(lambda: window_copy(WEST, True, ix - 1).wait_send())
-    pl.when((ix > 0) & (ix <= half))(lambda: window_copy(WEST, False, ix - 1).wait_send())
-    pl.when(ix == half - 1)(lambda: window_copy(EAST, True, ix + 1).wait_send())
-    pl.when((ix >= half) & (ix < X - 1))(lambda: window_copy(EAST, False, ix + 1).wait_send())
+    for j in range(H):
+        pl.when(ix > 0)(lambda: halo_copy(True, j).wait_send())
+        pl.when(ix < X - 1)(lambda: halo_copy(False, j).wait_send())
+    pl.when(ix == half + 1)(lambda: window_copy(WEST, 3, ix - 1).wait_send())
+    pl.when(ix == half - 1)(lambda: window_copy(EAST, 3, ix + 1).wait_send())
+    for c in range(4):
+        pl.when((ix > 0) & (ix <= half))(lambda: window_copy(WEST, c, ix - 1).wait_send())
+        pl.when((ix >= half) & (ix < X - 1))(lambda: window_copy(EAST, c, ix + 1).wait_send())
     for side in (0, 1):
         pl.when(outer & has_col[side])(lambda: wt_copy(side).wait_send())
     co_each(lambda copy: copy.wait_send())
@@ -520,16 +609,13 @@
     W = C + T
     top = N + 2 * H
     per = N // 3
-    deep = -(-LEV // 16) * 16
-    hi = lax.reduce_precision(column_mix, 8, 7)
-    hi, lo = (jnp.pad(x, ((0, deep - LEV), (0, deep - LEV))) for x in (hi, column_mix - hi))
-    mixer = jnp.concatenate([hi, lo, hi], axis=1).astype(BF16)
-    wx, wy = 0.5 * wind_x, 0.5 * wind_y
-    coef = jnp.stack([0.125 - wx, 0.125 + wx, 0.125 - wy, 0.125 + wy])
-    coef = jnp.broadcast_to(coef[:, :, None], (4, LEV, T))
+    deep = -(-3 * LEV // T) * T
+    LEVP = -(-LEV // 16) * 16
     vmem = pl.BlockSpec(memory_space=pltpu.VMEM)
+    hbm = pl.BlockSpec(memory_space=pltpu.HBM)
     smem = pl.BlockSpec(memory_space=pltpu.SMEM)
     V = lambda *s: pltpu.VMEM(s, F32)
+    I = lambda *s: pltpu.VMEM(s, jnp.int32)
     D = lambda *s: pltpu.SemaphoreType.DMA(s)
     outs = pl.pallas_call(
         functools.partial(kernel, X, Y, CY),
@@ -537,9 +623,22 @@
             jax.ShapeDtypeStruct((3, R, LEV, T), F32),
             jax.ShapeDtypeStruct((3, N, LEV, C), F32),
         ),
-        in_specs=[vmem, vmem, smem, vmem, vmem, vmem, vmem, vmem],
+        in_specs=[hbm, hbm, smem, hbm, hbm, hbm, hbm, hbm, hbm],
         out_specs=(vmem, vmem),
         scratch_shapes=[
+            V(3, LEV, R, T),
+            V(3, N, LEV, C),
+            I(4, 2, 4, C),
+            I(4, 2, 4, C),
+            V(4, 2, 4, C),
+            V(1, LEV),
+            V(1, LEV),
+            V(LEV, LEV),
+            V(3, R, LEV, T),
+            V(4, LEV, T),
+            V(3, LEVP, deep),
+            pltpu.VMEM((LEVP, deep), BF16),
+            pltpu.VMEM((3, 2 * T, W), BF16),
             V(2, LEV, T),
             V(3, 2, LEV, T),
             V(2, 3, LEV, T),
@@ -560,21 +659,23 @@
             V(4, 3, LEV, W),
             V(per, 3, LEV, T),
             V(per * X, 3, LEV, T),
-            D(3, 2), D(3, 2), D(2), D(2), D(2), D(2), D(2), D(2), D(2), D(2), D(X // 2, per), D(per * X),
+            D(8),
+            D(3, 2), D(3, 2), D(2), D(2), D(2, H), D(2, H), D(2, 4), D(2, 4), D(2), D(2), D(X // 2, per), D(per * X),
         ],
         compiler_params=pltpu.CompilerParams(
             collective_id=0, has_side_effects=True, vmem_limit_bytes=48 * 1024 * 1024
         ),
         cost_estimate=pl.CostEstimate(flops=200_000_000, bytes_accessed=6_000_000, transcendentals=0),
     )(
-        parent.transpose(0, 2, 1, 3),
+        parent,
         nest.transpose(0, 2, 1, 3),
         nest_anchor,
         donor_rows,
         donor_cols,
         donor_weights,
-        coef,
-        mixer,
+        wind_x.reshape(1, LEV),
+        wind_y.reshape(1, LEV),
+        column_mix,
     )
     return tuple(x.transpose(0, 2, 1, 3) for x in outs)
 

time: 56.9 us -> 55.4 us (0.974)
  other arithmetic: 2.24 us -> 0 us
  local copies, waits for them, and re-layouts: 6.43 us -> 8.36 us
  Pallas kernels: 46.4 us -> 45 us
    unnamed x11 -> x18, local copies, waits for them, and re-layouts: 6.35 us -> 8.36 us
    pallas_call x1, Pallas kernels: 46.4 us -> 45 us  [shards(): pl.pallas_call(functools.partial(kernel, X, Y, CY), out_shape=(jax.ShapeD...]
    another operation x3 -> x0, other arithmetic: 1.42 us -> none
    reduce_precision x1 -> x0, other arithmetic: 0.73 us -> none  [shards(): hi = lax.reduce_precision(column_mix, 8, 7)]
where the time goes in v2:
time: 55.4 us; the launch traced here: 54.6 us
  Pallas kernels  45 us (81%)
  local copies, waits for them, and re-layouts  8.36 us (15%)
  between operations  1.3 us (2%)
    pallas_call x1, Pallas kernels, shards(): pl.pallas_call(functools.partial(kernel, X, Y, CY), out_shape=(jax.ShapeD...  45 us
    unnamed x18, local copies, waits for them, and re-layouts  8.36 us

profile of v2, /device:TPU:18, one launch (start us, length us, event | category | flops | bytes accessed | tf_op | source)
XLA Modules:
  0.0 54.6 jit_solution(13187350018462202985)
XLA Ops:
  1.3 0.0 copy-start
  1.3 1.2 %copy-done = f32[3,40,6,384]{3,1,2,0:T(8,128)S(1)} copy-done((f32[3,40,6,384]{3,1,2,0:T(8,128)S(1)}, f32[3,40,6,384]{3,1,2,0:T(8,128)}, u32[]{:S(2)}) %copy-start) | copy-done | bytes 1105944
  2.5 0.0 copy-start.1
  2.5 0.9 %copy-done.1 = f32[3,40,4,128]{3,2,1,0:T(4,128)S(1)} copy-done((f32[3,40,4,128]{3,2,1,0:T(4,128)S(1)}, f32[3,40,4,128]{3,2,1,0:T(4,128)}, u32[]{:S(2)}) %copy-start.1) | copy-done | bytes 245784
  3.5 0.0 copy-start.2
  3.5 0.8 %copy-done.2 = s32[4,2,4,384]{3,2,1,0:T(4,128)S(1)} copy-done((s32[4,2,4,384]{3,2,1,0:T(4,128)S(1)}, s32[4,2,4,384]{3,2,1,0:T(4,128)}, u32[]{:S(2)}) %copy-start.2) | copy-done | bytes 49176
  4.3 0.0 copy-start.3
  4.3 0.8 %copy-done.3 = s32[4,2,4,384]{3,2,1,0:T(4,128)S(1)} copy-done((s32[4,2,4,384]{3,2,1,0:T(4,128)S(1)}, s32[4,2,4,384]{3,2,1,0:T(4,128)}, u32[]{:S(2)}) %copy-start.3) | copy-done | bytes 49176
  5.1 0.0 copy-start.4
  5.1 0.8 %copy-done.4 = f32[4,2,4,384]{3,2,1,0:T(4,128)S(1)} copy-done((f32[4,2,4,384]{3,2,1,0:T(4,128)S(1)}, f32[4,2,4,384]{3,2,1,0:T(4,128)}, u32[]{:S(2)}) %copy-start.4) | copy-done | bytes 49176
  5.9 0.0 copy-start.5
  5.9 0.7 %copy-done.5 = f32[40,40]{1,0:T(8,128)S(1)} copy-done((f32[40,40]{1,0:T(8,128)S(1)}, f32[40,40]{1,0:T(8,128)}, u32[]{:S(2)}) %copy-start.5) | copy-done | bytes 6424
  6.6 0.0 copy-start.6
  6.6 0.7 %copy-done.6 = f32[40]{0:T(128)S(1)} copy-done((f32[40]{0:T(128)S(1)}, f32[40]{0:T(128)}, u32[]{:S(2)}) %copy-start.6) | copy-done | bytes 184
  7.2 0.0 copy-start.7
  7.3 0.7 %copy-done.7 = f32[40]{0:T(128)S(1)} copy-done((f32[40]{0:T(128)S(1)}, f32[40]{0:T(128)}, u32[]{:S(2)}) %copy-start.7) | copy-done | bytes 184
  7.9 45.0 %shard_map.104 = (f32[3,4,40,128]{3,2,1,0:T(8,128)S(1)}, f32[3,6,40,384]{3,2,1,0:T(8,128)S(1)}) custom-call(f32[3,40,4,128]{3,2,1,0:T(4,128)S(1)} %copy-done.1, f32[3,6,40,384]{3,2,1,0:T(8,128)S(1)} %bitcast.5, s32[1]{0:T(128)S(6)} %copy.13.anchor, s32[4,2,4,384]{3,2,1,0:T(4,128)S(1)} %copy-done.2, s32[4,2,4,384]{3,2,1,0:T(4,128)S(1)} %copy-done.3, ...), custom_call_target="tpu_custom_call" | custom-call | flops 200000000 | bytes 6000000 | tf_op jit(solution)/shard_map/pallas_call | solution.py:620
  52.9 0.8 %copy.11 = f32[3,40,4,128]{3,2,1,0:T(4,128)} copy(f32[3,40,4,128]{3,1,2,0:T(8,128)S(1)} %bitcast.7) | data formatting | bytes 491520
  53.6 1.0 %copy.14 = f32[3,40,6,384]{3,1,2,0:T(8,128)} copy(f32[3,40,6,384]{3,1,2,0:T(8,128)S(1)} %bitcast.6) | data formatting | bytes 2211840
Async XLA Ops:
  1.3 1.2 %copy-start = (f32[3,40,6,384]{3,1,2,0:T(8,128)S(1)}, f32[3,40,6,384]{3,1,2,0:T(8,128)}, u32[]{:S(2)}) copy-start(f32[3,40,6,384]{3,1,2,0:T(8,128)} %param.10) | copy-start | bytes 3317764
  2.5 0.9 %copy-start.1 = (f32[3,40,4,128]{3,2,1,0:T(4,128)S(1)}, f32[3,40,4,128]{3,2,1,0:T(4,128)}, u32[]{:S(2)}) copy-start(f32[3,40,4,128]{3,2,1,0:T(4,128)} %parent_in.1) | copy-start | bytes 737284
  3.5 0.8 %copy-start.2 = (s32[4,2,4,384]{3,2,1,0:T(4,128)S(1)}, s32[4,2,4,384]{3,2,1,0:T(4,128)}, u32[]{:S(2)}) copy-start(s32[4,2,4,384]{3,2,1,0:T(4,128)} %rows_in.1) | copy-start | bytes 147460
  4.3 0.8 %copy-start.3 = (s32[4,2,4,384]{3,2,1,0:T(4,128)S(1)}, s32[4,2,4,384]{3,2,1,0:T(4,128)}, u32[]{:S(2)}) copy-start(s32[4,2,4,384]{3,2,1,0:T(4,128)} %cols_in.1) | copy-start | bytes 147460
  5.1 0.8 %copy-start.4 = (f32[4,2,4,384]{3,2,1,0:T(4,128)S(1)}, f32[4,2,4,384]{3,2,1,0:T(4,128)}, u32[]{:S(2)}) copy-start(f32[4,2,4,384]{3,2,1,0:T(4,128)} %wts_in.1) | copy-start | bytes 147460
  5.9 0.7 %copy-start.5 = (f32[40,40]{1,0:T(8,128)S(1)}, f32[40,40]{1,0:T(8,128)}, u32[]{:S(2)}) copy-start(f32[40,40]{1,0:T(8,128)} %mix_in.1) | copy-start | bytes 19204
  6.6 0.7 %copy-start.6 = (f32[40]{0:T(128)S(1)}, f32[40]{0:T(128)}, u32[]{:S(2)}) copy-start(f32[40]{0:T(128)} %param.15) | copy-start | bytes 484
  7.2 0.7 %copy-start.7 = (f32[40]{0:T(128)S(1)}, f32[40]{0:T(128)}, u32[]{:S(2)}) copy-start(f32[40]{0:T(128)} %param.16) | copy-start | bytes 484

commit v3 on v2

--- a/solution.py
+++ b/solution.py
@@ -86,31 +86,31 @@
                 )
 
     lane = lanes((LEV, T))
-    loads[0].wait()
     loads[1].wait()
     for k in range(3):
         for r in range(R):
             parent[k, r] = raw[k, :, r, :]
-    edge[...] = jnp.zeros_like(edge)
-
-    def pack_nest(n, carry):
-        spot = (lane >= H * n) & (lane < H * n + H)
-        k, r = n // N, lax.rem(n, N)
-        left = nest[k, r, :, 0:T]
-        right = nest[k, r, :, C - T : C]
-        edge[0] = jnp.where(spot, pltpu.roll(left, H * n, 1), edge[0])
-        edge[1] = jnp.where(spot, pltpu.roll(right, lax.rem(H * n + H, T), 1), edge[1])
-        return carry
-
-    def pack_parent(n, carry):
-        spot = (lane >= 64 + H * n) & (lane < 64 + H * n + H)
-        v = parent[n // R, lax.rem(n, R)]
-        edge[0] = jnp.where(spot, pltpu.roll(v, 64 + H * n, 1), edge[0])
-        edge[1] = jnp.where(spot, pltpu.roll(v, 64 + H * n + H, 1), edge[1])
-        return carry
-
-    lax.fori_loop(0, 3 * N, pack_nest, 0)
-    lax.fori_loop(0, 3 * R, pack_parent, 0)
+
+    a0 = jnp.full((LEV, T), anchor[0], jnp.int32)
+    first = (a0 - 1, a0 + (R * X // 2 - 4 - 1))
+    in_west = ix <= half + 1
+    in_east = ix >= half - 1
+
+    def share_rows(which):
+        base = 1 if which else 0
+
+        def one(n, carry):
+            t, k = n // 3, lax.rem(n, 3)
+            body = jnp.zeros((LEV, T), F32)
+            for i in range(R):
+                body = jnp.where(first[which] + t == R * ix + i, parent[k, i], body)
+            send_w[which, base + n] = body
+            return carry
+
+        lax.fori_loop(0, 18, one, 0)
+
+    pl.when(in_west)(lambda: share_rows(WEST))
+    pl.when(in_east)(lambda: share_rows(EAST))
 
     pl.semaphore_wait(barrier, near)
 
@@ -127,13 +127,57 @@
 
     def halo_copy(down, j):
         if down:
-            return rcopy(nest.at[:, j], hh.at[:, j], halo_ss.at[1, j], halo_rs.at[1, j], ix - 1, iy)
+            return rcopy(nest_in.at[:, j], hh.at[:, j], halo_ss.at[1, j], halo_rs.at[1, j], ix - 1, iy)
         i = H - 1 - j
-        return rcopy(nest.at[:, N - 1 - j], hl.at[:, i], halo_ss.at[0, j], halo_rs.at[0, j], ix + 1, iy)
+        return rcopy(nest_in.at[:, N - 1 - j], hl.at[:, i], halo_ss.at[0, j], halo_rs.at[0, j], ix + 1, iy)
 
     def halo_send(down, rows):
         for j in rows:
             halo_copy(down, j).start()
+
+    spans = (((0, 6), (6, 12), (12, 15), (15, 19)), ((13, 19), (7, 13), (4, 7), (0, 4)))
+
+    def window_copy(which, c, x):
+        lo, hi = spans[which][c]
+        span = pl.ds(lo, hi - lo)
+        return rcopy(
+            send_w.at[which, span], recv_w.at[which, span], win_ss.at[which, c], win_rs.at[which, c], x, iy
+        )
+
+    def window_add(which, c):
+        window_copy(which, c, lax.rem(ix + 1, X)).wait_recv()
+
+        def add(n, carry):
+            send_w[which, n] = send_w[which, n] + recv_w[which, n]
+            return carry
+
+        lax.fori_loop(spans[which][c][0], spans[which][c][1], add, 0)
+
+    @pl.when(ix == half)
+    def _():
+        for c in range(3):
+            window_copy(WEST, c, ix - 1).start()
+            if half < X - 1:
+                window_copy(EAST, c, ix + 1).start()
+
+    pl.when(ix > 0)(lambda: halo_send(True, (0,)))
+    pl.when(ix < X - 1)(lambda: halo_send(False, (0,)))
+
+    loads[0].wait()
+    for side in (0, 1):
+        packs = jnp.zeros((LEV, T), F32)
+        for n in range(3 * N + 3 * R):
+            if n < 3 * N:
+                v = nest[n // N, n % N, :, C - T : C] if side else nest[n // N, n % N, :, 0:T]
+                to = H * n
+            else:
+                m = n - 3 * N
+                v = parent[m // R, m % R]
+                to = 64 + H * m
+            spot = (lane >= to) & (lane < to + H)
+            turn = (to + H * side) % T
+            packs = jnp.where(spot, pltpu.roll(v, turn, 1) if turn else v, packs)
+        edge[side] = packs
 
     for dx in (0, -1, 1):
         for side in (0, 1):
@@ -144,10 +188,8 @@
             )
     pl.when(ix > 0)(lambda: ph_copy(True).start())
     pl.when(ix < X - 1)(lambda: ph_copy(False).start())
-    pl.when(ix > 0)(lambda: halo_send(True, (0,)))
-    pl.when(ix < X - 1)(lambda: halo_send(False, (0,)))
-    pl.when(ix > half)(lambda: halo_send(True, (1, 2)))
-    pl.when(ix < half)(lambda: halo_send(False, (1, 2)))
+    pl.when(ix > half + 1)(lambda: halo_send(True, (1, 2)))
+    pl.when(ix < half - 1)(lambda: halo_send(False, (1, 2)))
 
     def pack_wait(dx):
         for side in (0, 1):
@@ -172,58 +214,44 @@
 
     lax.fori_loop(0, 3 * R, take_parent, 0)
 
-    a0 = jnp.full((LEV, T), anchor[0], jnp.int32)
-    first = (a0 - 1, a0 + (R * X // 2 - 4 - 1))
-
-    def share(which):
-        base = 1 if which else 0
-        rims = 0 if which else 18
-
-        def one(n, acc):
-            t, k = n // 3, lax.rem(n, 3)
-            body = jnp.zeros((LEV, T), F32)
+    def share_rims(which):
+        acc = jnp.zeros((LEV, T), F32)
+        for n in range(18):
+            t, k = n // 3, n % 3
             rim = jnp.zeros((LEV, T), F32)
             for i in range(R):
-                hit = first[which] + t == R * ix + i
-                body = jnp.where(hit, px[k, i + 1, :, 0:T], body)
-                rim = jnp.where(hit, px[k, i + 1, :, T : 2 * T], rim)
-            send_w[which, base + n] = body
+                rim = jnp.where(first[which] + t == R * ix + i, px[k, i + 1, :, T : 2 * T], rim)
             spot = (lane >= 6 * n) & (lane < 6 * n + 6)
-            return jnp.where(spot, pltpu.roll(rim, lax.rem(6 * n + H, T), 1), acc)
-
-        send_w[which, rims] = lax.fori_loop(0, 18, one, jnp.zeros((LEV, T), F32))
-
-    in_west = ix <= half + 1
-    in_east = ix >= half - 1
-    pl.when(in_west)(lambda: share(WEST))
-    pl.when(in_east)(lambda: share(EAST))
-
-    spans = (((0, 6), (6, 12), (12, 15), (15, 19)), ((13, 19), (7, 13), (4, 7), (0, 4)))
-
-    def window_copy(which, c, x):
-        lo, hi = spans[which][c]
-        span = pl.ds(lo, hi - lo)
-        return rcopy(
-            send_w.at[which, span], recv_w.at[which, span], win_ss.at[which, c], win_rs.at[which, c], x, iy
-        )
-
-    def window_add(which, c):
-        window_copy(which, c, lax.rem(ix + 1, X)).wait_recv()
-
-        def add(n, carry):
-            send_w[which, n] = send_w[which, n] + recv_w[which, n]
-            return carry
-
-        lax.fori_loop(spans[which][c][0], spans[which][c][1], add, 0)
-
-    pl.when(ix == half + 1)(lambda: window_copy(WEST, 3, ix - 1).start())
-    pl.when(ix == half - 1)(lambda: window_copy(EAST, 3, ix + 1).start())
-
-    @pl.when(ix == half)
-    def _():
-        for c in range(3):
-            window_copy(WEST, c, ix - 1).start()
-            if half < X - 1:
+            acc = jnp.where(spot, pltpu.roll(rim, (6 * n + H) % T, 1), acc)
+        send_w[which, 0 if which else 18] = acc
+
+    pl.when(in_west)(lambda: share_rims(WEST))
+    pl.when(in_east)(lambda: share_rims(EAST))
+
+    @pl.when(ix == half + 1)
+    def _():
+        window_copy(WEST, 3, ix - 1).start()
+        halo_send(True, (1, 2))
+
+    @pl.when(ix == half - 1)
+    def _():
+        window_copy(EAST, 3, ix + 1).start()
+        halo_send(False, (1, 2))
+
+    if half > 1:
+
+        @pl.when((ix > 0) & (ix < half))
+        def _():
+            for c in range(3):
+                window_add(WEST, c)
+                window_copy(WEST, c, ix - 1).start()
+
+    if half + 1 < X - 1:
+
+        @pl.when((ix > half) & (ix < X - 1))
+        def _():
+            for c in range(3):
+                window_add(EAST, c)
                 window_copy(EAST, c, ix + 1).start()
 
     def take_rows(src, dx, first_row, count, at, only=None):
@@ -253,17 +281,15 @@
 
         @pl.when((ix > 0) & (ix < half))
         def _():
-            for c in range(4):
-                window_add(WEST, c)
-                window_copy(WEST, c, ix - 1).start()
+            window_add(WEST, 3)
+            window_copy(WEST, 3, ix - 1).start()
 
     if half + 1 < X - 1:
 
         @pl.when((ix > half) & (ix < X - 1))
         def _():
-            for c in range(4):
-                window_add(EAST, c)
-                window_copy(EAST, c, ix + 1).start()
+            window_add(EAST, 3)
+            window_copy(EAST, 3, ix + 1).start()
 
     pl.when((ix > 0) & (ix <= half))(lambda: halo_send(True, (1, 2)))
     pl.when((ix < X - 1) & (ix >= half))(lambda: halo_send(False, (1, 2)))
@@ -663,7 +689,7 @@
             D(3, 2), D(3, 2), D(2), D(2), D(2, H), D(2, H), D(2, 4), D(2, 4), D(2), D(2), D(X // 2, per), D(per * X),
         ],
         compiler_params=pltpu.CompilerParams(
-            collective_id=0, has_side_effects=True, vmem_limit_bytes=48 * 1024 * 1024
+            collective_id=0, has_side_effects=True, vmem_limit_bytes=62 * 1024 * 1024
         ),
         cost_estimate=pl.CostEstimate(flops=200_000_000, bytes_accessed=6_000_000, transcendentals=0),
     )(

time: 55.4 us -> 45.1 us (0.81)
  Pallas kernels: 45 us -> 39.4 us
  local copies, waits for them, and re-layouts: 8.36 us -> 4 us
    pallas_call x1, Pallas kernels: 45 us -> 39.4 us  [shards(): pl.pallas_call(functools.partial(kernel, X, Y, CY), out_shape=(jax.ShapeD...]
    unnamed x18 -> x2, local copies, waits for them, and re-layouts: 8.36 us -> 4 us
where the time goes in v3:
time: 45.1 us; the launch traced here: 44.7 us
  Pallas kernels  39.4 us (87%)
  local copies, waits for them, and re-layouts  4 us (9%)
  between operations  1.29 us (3%)
    pallas_call x1, Pallas kernels, shards(): pl.pallas_call(functools.partial(kernel, X, Y, CY), out_shape=(jax.ShapeD...  39.4 us
    unnamed x2, local copies, waits for them, and re-layouts  4 us

profile of v3, /device:TPU:18, one launch (start us, length us, event | category | flops | bytes accessed | tf_op | source)
XLA Modules:
  0.0 44.7 jit_solution(11551580269463446155)
XLA Ops:
  1.3 39.4 %shard_map.104 = (f32[3,4,40,128]{3,2,1,0:T(8,128)}, f32[3,6,40,384]{3,2,1,0:T(8,128)}) custom-call(f32[3,40,4,128]{3,2,1,0:T(4,128)} %parent_in.1, f32[3,6,40,384]{3,2,1,0:T(8,128)} %bitcast.5, s32[1]{0:T(128)S(6)} %copy.13.anchor, s32[4,2,4,384]{3,2,1,0:T(4,128)} %rows_in.1, s32[4,2,4,384]{3,2,1,0:T(4,128)} %cols_in.1, f32[4,2,4,384]{3,2,1,0:T(4,128)} %wts_in.1, ...), custom_call_target="tpu_custom_call" | custom-call | flops 200000000 | bytes 6000000 | tf_op jit(solution)/shard_map/pallas_call | solution.py:646
  40.7 1.7 %copy.11 = f32[3,40,4,128]{3,2,1,0:T(4,128)} copy(f32[3,40,4,128]{3,1,2,0:T(8,128)} %bitcast.7) | data formatting | bytes 491520
  42.4 2.3 %copy.14 = f32[3,40,6,384]{3,1,2,0:T(8,128)} copy(f32[3,40,6,384]{3,1,2,0:T(8,128)} %bitcast.6) | data formatting | bytes 2211840

commit v4 on v3

--- a/solution.py
+++ b/solution.py
@@ -112,57 +112,6 @@
     pl.when(in_west)(lambda: share_rows(WEST))
     pl.when(in_east)(lambda: share_rows(EAST))
 
-    pl.semaphore_wait(barrier, near)
-
-    def pack_copy(side, dx):
-        return rcopy(
-            edge.at[side], pb.at[1 - dx, 1 - side], pack_ss.at[dx + 1, side], pack_rs.at[1 - dx, 1 - side],
-            ix + dx, col_partner(side),
-        )
-
-    def ph_copy(down):
-        if down:
-            return rcopy(parent.at[:, 0], phb.at[1], ph_ss.at[1], ph_rs.at[1], ix - 1, iy)
-        return rcopy(parent.at[:, R - 1], phb.at[0], ph_ss.at[0], ph_rs.at[0], ix + 1, iy)
-
-    def halo_copy(down, j):
-        if down:
-            return rcopy(nest_in.at[:, j], hh.at[:, j], halo_ss.at[1, j], halo_rs.at[1, j], ix - 1, iy)
-        i = H - 1 - j
-        return rcopy(nest_in.at[:, N - 1 - j], hl.at[:, i], halo_ss.at[0, j], halo_rs.at[0, j], ix + 1, iy)
-
-    def halo_send(down, rows):
-        for j in rows:
-            halo_copy(down, j).start()
-
-    spans = (((0, 6), (6, 12), (12, 15), (15, 19)), ((13, 19), (7, 13), (4, 7), (0, 4)))
-
-    def window_copy(which, c, x):
-        lo, hi = spans[which][c]
-        span = pl.ds(lo, hi - lo)
-        return rcopy(
-            send_w.at[which, span], recv_w.at[which, span], win_ss.at[which, c], win_rs.at[which, c], x, iy
-        )
-
-    def window_add(which, c):
-        window_copy(which, c, lax.rem(ix + 1, X)).wait_recv()
-
-        def add(n, carry):
-            send_w[which, n] = send_w[which, n] + recv_w[which, n]
-            return carry
-
-        lax.fori_loop(spans[which][c][0], spans[which][c][1], add, 0)
-
-    @pl.when(ix == half)
-    def _():
-        for c in range(3):
-            window_copy(WEST, c, ix - 1).start()
-            if half < X - 1:
-                window_copy(EAST, c, ix + 1).start()
-
-    pl.when(ix > 0)(lambda: halo_send(True, (0,)))
-    pl.when(ix < X - 1)(lambda: halo_send(False, (0,)))
-
     loads[0].wait()
     for side in (0, 1):
         packs = jnp.zeros((LEV, T), F32)
@@ -179,6 +128,47 @@
             packs = jnp.where(spot, pltpu.roll(v, turn, 1) if turn else v, packs)
         edge[side] = packs
 
+    pl.semaphore_wait(barrier, near)
+
+    def pack_copy(side, dx):
+        return rcopy(
+            edge.at[side], pb.at[1 - dx, 1 - side], pack_ss.at[dx + 1, side], pack_rs.at[1 - dx, 1 - side],
+            ix + dx, col_partner(side),
+        )
+
+    def ph_copy(down):
+        if down:
+            return rcopy(parent.at[:, 0], phb.at[1], ph_ss.at[1], ph_rs.at[1], ix - 1, iy)
+        return rcopy(parent.at[:, R - 1], phb.at[0], ph_ss.at[0], ph_rs.at[0], ix + 1, iy)
+
+    def halo_copy(down, j):
+        if down:
+            return rcopy(nest_in.at[:, j], hh.at[:, j], halo_ss.at[1, j], halo_rs.at[1, j], ix - 1, iy)
+        i = H - 1 - j
+        return rcopy(nest_in.at[:, N - 1 - j], hl.at[:, i], halo_ss.at[0, j], halo_rs.at[0, j], ix + 1, iy)
+
+    def halo_send(down, rows):
+        for j in rows:
+            halo_copy(down, j).start()
+
+    spans = (((0, 6), (6, 12), (12, 15), (15, 19)), ((13, 19), (7, 13), (4, 7), (0, 4)))
+
+    def window_copy(which, c, x):
+        lo, hi = spans[which][c]
+        span = pl.ds(lo, hi - lo)
+        return rcopy(
+            send_w.at[which, span], recv_w.at[which, span], win_ss.at[which, c], win_rs.at[which, c], x, iy
+        )
+
+    def window_add(which, c):
+        window_copy(which, c, lax.rem(ix + 1, X)).wait_recv()
+
+        def add(n, carry):
+            send_w[which, n] = send_w[which, n] + recv_w[which, n]
+            return carry
+
+        lax.fori_loop(spans[which][c][0], spans[which][c][1], add, 0)
+
     for dx in (0, -1, 1):
         for side in (0, 1):
             there = has_col[side] & row_ok(dx)
@@ -188,6 +178,16 @@
             )
     pl.when(ix > 0)(lambda: ph_copy(True).start())
     pl.when(ix < X - 1)(lambda: ph_copy(False).start())
+    @pl.when(ix == half)
+    def _():
+        for c in range(3):
+            window_copy(WEST, c, ix - 1).start()
+            if half < X - 1:
+                window_copy(EAST, c, ix + 1).start()
+
+    starter = (ix == half + 1) | (ix == half - 1)
+    pl.when((ix > 0) & jnp.logical_not(starter))(lambda: halo_send(True, (0,)))
+    pl.when((ix < X - 1) & jnp.logical_not(starter))(lambda: halo_send(False, (0,)))
     pl.when(ix > half + 1)(lambda: halo_send(True, (1, 2)))
     pl.when(ix < half - 1)(lambda: halo_send(False, (1, 2)))
 
@@ -231,12 +231,14 @@
     @pl.when(ix == half + 1)
     def _():
         window_copy(WEST, 3, ix - 1).start()
-        halo_send(True, (1, 2))
+        halo_send(True, (0, 1, 2))
+        pl.when(ix < X - 1)(lambda: halo_send(False, (0,)))
 
     @pl.when(ix == half - 1)
     def _():
         window_copy(EAST, 3, ix + 1).start()
-        halo_send(False, (1, 2))
+        pl.when(ix > 0)(lambda: halo_send(True, (0,)))
+        halo_send(False, (0, 1, 2))
 
     if half > 1:
 
@@ -637,6 +639,7 @@
     per = N // 3
     deep = -(-3 * LEV // T) * T
     LEVP = -(-LEV // 16) * 16
+    keep = lambda x: pltpu.with_memory_space_constraint(x, pltpu.HBM)
     vmem = pl.BlockSpec(memory_space=pltpu.VMEM)
     hbm = pl.BlockSpec(memory_space=pltpu.HBM)
     smem = pl.BlockSpec(memory_space=pltpu.SMEM)
@@ -646,8 +649,8 @@
     outs = pl.pallas_call(
         functools.partial(kernel, X, Y, CY),
         out_shape=(
-            jax.ShapeDtypeStruct((3, R, LEV, T), F32),
-            jax.ShapeDtypeStruct((3, N, LEV, C), F32),
+            pltpu.VMEM((3, R, LEV, T), F32),
+            pltpu.VMEM((3, N, LEV, C), F32),
         ),
         in_specs=[hbm, hbm, smem, hbm, hbm, hbm, hbm, hbm, hbm],
         out_specs=(vmem, vmem),
@@ -689,19 +692,19 @@
             D(3, 2), D(3, 2), D(2), D(2), D(2, H), D(2, H), D(2, 4), D(2, 4), D(2), D(2), D(X // 2, per), D(per * X),
         ],
         compiler_params=pltpu.CompilerParams(
-            collective_id=0, has_side_effects=True, vmem_limit_bytes=62 * 1024 * 1024
+            collective_id=0, has_side_effects=True, vmem_limit_bytes=48 * 1024 * 1024
         ),
         cost_estimate=pl.CostEstimate(flops=200_000_000, bytes_accessed=6_000_000, transcendentals=0),
     )(
-        parent,
-        nest.transpose(0, 2, 1, 3),
+        keep(parent),
+        keep(nest.transpose(0, 2, 1, 3)),
         nest_anchor,
-        donor_rows,
-        donor_cols,
-        donor_weights,
-        wind_x.reshape(1, LEV),
-        wind_y.reshape(1, LEV),
-        column_mix,
+        keep(donor_rows),
+        keep(donor_cols),
+        keep(donor_weights),
+        keep(wind_x.reshape(1, LEV)),
+        keep(wind_y.reshape(1, LEV)),
+        keep(column_mix),
     )
     return tuple(x.transpose(0, 2, 1, 3) for x in outs)
 

time: 45.1 us -> 42 us (0.931)
  local copies, waits for them, and re-layouts: 4 us -> 1.75 us
  Pallas kernels: 39.4 us -> 38.8 us
    unnamed x2, local copies, waits for them, and re-layouts: 4 us -> 1.75 us
    pallas_call x1, Pallas kernels: 39.4 us -> 38.8 us  [shards(): pl.pallas_call(functools.partial(kernel, X, Y, CY), out_shape=(pltpu.VMEM...]
where the time goes in v4:
time: 42 us; the launch traced here: 41.8 us
  Pallas kernels  38.8 us (92%)
  local copies, waits for them, and re-layouts  1.75 us (4%)
  between operations  1.29 us (3%)
    pallas_call x1, Pallas kernels, shards(): pl.pallas_call(functools.partial(kernel, X, Y, CY), out_shape=(pltpu.VMEM...  38.8 us
    unnamed x2, local copies, waits for them, and re-layouts  1.75 us

profile of v4, /device:TPU:18, one launch (start us, length us, event | category | flops | bytes accessed | tf_op | source)
XLA Modules:
  0.0 41.8 jit_solution(9578844601683212836)
XLA Ops:
  1.3 38.8 %shard_map.104 = (f32[3,4,40,128]{3,2,1,0:T(8,128)S(1)}, f32[3,6,40,384]{3,2,1,0:T(8,128)S(1)}) custom-call(f32[3,40,4,128]{3,2,1,0:T(4,128)} %parent_in.1, f32[3,6,40,384]{3,2,1,0:T(8,128)} %bitcast.7, s32[1]{0:T(128)S(6)} %copy.14.anchor, s32[4,2,4,384]{3,2,1,0:T(4,128)} %rows_in.1, s32[4,2,4,384]{3,2,1,0:T(4,128)} %cols_in.1, f32[4,2,4,384]{3,2,1,0:T(4,128)} %wts_in.1, ...), custom_call_target="tpu_custom_call" | custom-call | flops 200000000 | bytes 6000000 | tf_op jit(solution)/shard_map/pallas_call | solution.py:649
  40.1 0.8 %copy.11 = f32[3,40,4,128]{3,2,1,0:T(4,128)} copy(f32[3,40,4,128]{3,1,2,0:T(8,128)S(1)} %bitcast.6) | data formatting | bytes 491520
  40.8 1.0 %copy.13 = f32[3,40,6,384]{3,1,2,0:T(8,128)} copy(f32[3,40,6,384]{3,1,2,0:T(8,128)S(1)} %bitcast.5) | data formatting | bytes 2211840

commit v5 on v4

--- a/solution.py
+++ b/solution.py
@@ -185,11 +185,12 @@
             if half < X - 1:
                 window_copy(EAST, c, ix + 1).start()
 
-    starter = (ix == half + 1) | (ix == half - 1)
-    pl.when((ix > 0) & jnp.logical_not(starter))(lambda: halo_send(True, (0,)))
-    pl.when((ix < X - 1) & jnp.logical_not(starter))(lambda: halo_send(False, (0,)))
-    pl.when(ix > half + 1)(lambda: halo_send(True, (1, 2)))
-    pl.when(ix < half - 1)(lambda: halo_send(False, (1, 2)))
+    pl.when(ix > 0)(lambda: halo_send(True, (0,)))
+    pl.when(ix < X - 1)(lambda: halo_send(False, (0,)))
+    pl.when((ix > 0) & (ix != half) & (ix != half + 1))(lambda: halo_send(True, (1, 2)))
+    pl.when((ix < X - 1) & (ix != half) & (ix != half - 1))(lambda: halo_send(False, (1, 2)))
+    pl.when(ix == half)(lambda: halo_send(True, (1,)))
+    pl.when((ix == half) & (ix < X - 1))(lambda: halo_send(False, (1,)))
 
     def pack_wait(dx):
         for side in (0, 1):
@@ -231,14 +232,12 @@
     @pl.when(ix == half + 1)
     def _():
         window_copy(WEST, 3, ix - 1).start()
-        halo_send(True, (0, 1, 2))
-        pl.when(ix < X - 1)(lambda: halo_send(False, (0,)))
+        halo_send(True, (1, 2))
 
     @pl.when(ix == half - 1)
     def _():
         window_copy(EAST, 3, ix + 1).start()
-        pl.when(ix > 0)(lambda: halo_send(True, (0,)))
-        halo_send(False, (0, 1, 2))
+        halo_send(False, (1, 2))
 
     if half > 1:
 
@@ -293,8 +292,8 @@
             window_add(EAST, 3)
             window_copy(EAST, 3, ix + 1).start()
 
-    pl.when((ix > 0) & (ix <= half))(lambda: halo_send(True, (1, 2)))
-    pl.when((ix < X - 1) & (ix >= half))(lambda: halo_send(False, (1, 2)))
+    pl.when(ix == half)(lambda: halo_send(True, (2,)))
+    pl.when((ix == half) & (ix < X - 1))(lambda: halo_send(False, (2,)))
 
     for load in loads[2:5]:
         load.wait()

time: 42 us -> 45 us (1.071)
  Pallas kernels: 38.8 us -> 41.8 us
    pallas_call x1, Pallas kernels: 38.8 us -> 41.8 us  [shards(): pl.pallas_call(functools.partial(kernel, X, Y, CY), out_shape=(pltpu.VMEM...]
where the time goes in v5:
time: 45 us; the launch traced here: 44.8 us
  Pallas kernels  41.8 us (93%)
  local copies, waits for them, and re-layouts  1.75 us (4%)
  between operations  1.29 us (3%)
    pallas_call x1, Pallas kernels, shards(): pl.pallas_call(functools.partial(kernel, X, Y, CY), out_shape=(pltpu.VMEM...  41.8 us
    unnamed x2, local copies, waits for them, and re-layouts  1.75 us

profile of v5, /device:TPU:18, one launch (start us, length us, event | category | flops | bytes accessed | tf_op | source)
XLA Modules:
  0.0 44.8 jit_solution(13484501743926468534)
XLA Ops:
  1.3 41.8 %shard_map.104 = (f32[3,4,40,128]{3,2,1,0:T(8,128)S(1)}, f32[3,6,40,384]{3,2,1,0:T(8,128)S(1)}) custom-call(f32[3,40,4,128]{3,2,1,0:T(4,128)} %parent_in.1, f32[3,6,40,384]{3,2,1,0:T(8,128)} %bitcast.7, s32[1]{0:T(128)S(6)} %copy.14.anchor, s32[4,2,4,384]{3,2,1,0:T(4,128)} %rows_in.1, s32[4,2,4,384]{3,2,1,0:T(4,128)} %cols_in.1, f32[4,2,4,384]{3,2,1,0:T(4,128)} %wts_in.1, ...), custom_call_target="tpu_custom_call" | custom-call | flops 200000000 | bytes 6000000 | tf_op jit(solution)/shard_map/pallas_call | solution.py:648
  43.1 0.8 %copy.11 = f32[3,40,4,128]{3,2,1,0:T(4,128)} copy(f32[3,40,4,128]{3,1,2,0:T(8,128)S(1)} %bitcast.6) | data formatting | bytes 491520
  43.8 1.0 %copy.13 = f32[3,40,6,384]{3,1,2,0:T(8,128)} copy(f32[3,40,6,384]{3,1,2,0:T(8,128)S(1)} %bitcast.5) | data formatting | bytes 2211840
